TPU v7x, 32 devices: a whole 2x2x4 slice. The times are simulated.
32 devices in a mesh: rep: 2 (over core), fsdp: 16 (over z, y, x).
Axes of the slice: x: 2, y: 2, z: 4, core: 2. Of those that a mesh axis runs over, the one named last changes fastest.
Arguments:
- hidden_in: bfloat16 [4, 1024, 2048], P('rep', 'fsdp'), may hold values from -6 to 6
- cotangent: bfloat16 [4, 1024, 2048], P('rep', 'fsdp'), may hold values from -6 to 6
- lengths: int32 [4], P('rep'), may hold values from 256 to 1024, as said below
- routes: int32 [4, 1024, 6], P('rep', 'fsdp'), may hold values from 0 to 15, all different within a row; in each aligned block of 64 rows (0 to 63, 64 to 127, ..., all dimensions but the last counted through in order) at most 36 rows name the same one
- gate_values: float32 [4, 1024, 6], P('rep', 'fsdp'), may hold values from 0.25 to 1
- attn_gain: bfloat16 [2048], P('fsdp'), may hold values from 0.5 to 1.5
- query_proj: bfloat16 [2048, 3072], P('fsdp'), may hold values from -0.125 to 0.125
- latent_proj: bfloat16 [2048, 576], P('fsdp'), may hold values from -0.125 to 0.125
- latent_gain: bfloat16 [512], P('fsdp'), may hold values from 0.5 to 1.5
- expand_proj: bfloat16 [512, 4096], P('fsdp'), may hold values from -0.25 to 0.25
- output_proj: bfloat16 [2048, 2048], P('fsdp'), may hold values from -1.5 to 1.5
- ffn_gain: bfloat16 [2048], P('fsdp'), may hold values from 0.5 to 1.5
- shared_gate: bfloat16 [2048, 2816], P('fsdp'), may hold values from -0.125 to 0.125
- shared_lift: bfloat16 [2048, 2816], P('fsdp'), may hold values from -0.125 to 0.125
- shared_down: bfloat16 [2816, 2048], P('fsdp'), may hold values from -0.109375 to 0.109375
- expert_gate: bfloat16 [16, 2048, 1408], P('fsdp', None, 'rep'), may hold values from -0.125 to 0.125
- expert_lift: bfloat16 [16, 2048, 1408], P('fsdp', None, 'rep'), may hold values from -0.125 to 0.125
- expert_down: bfloat16 [16, 1408, 2048], P('fsdp', 'rep'), may hold values from -0.15625 to 0.15625
Outputs:
- block_out: bfloat16 [4, 1024, 2048], P('rep', 'fsdp')
- grad_hidden: bfloat16 [4, 1024, 2048], P('rep', 'fsdp')
- grad_attn_gain: float32 [2048], P('fsdp')
- grad_query_proj: float32 [2048, 3072], P('fsdp')
- grad_latent_proj: float32 [2048, 576], P('fsdp')
- grad_latent_gain: float32 [512], P('fsdp')
- grad_expand_proj: float32 [512, 4096], P('fsdp')
- grad_output_proj: float32 [2048, 2048], P('fsdp')
- grad_ffn_gain: float32 [2048], P('fsdp')
- grad_shared_gate: float32 [2048, 2816], P('fsdp')
- grad_shared_lift: float32 [2048, 2816], P('fsdp')
- grad_shared_down: float32 [2816, 2048], P('fsdp')
- grad_expert_gate: float32 [16, 2048, 1408], P('fsdp', None, 'rep')
- grad_expert_lift: float32 [16, 2048, 1408], P('fsdp', None, 'rep')
- grad_expert_down: float32 [16, 1408, 2048], P('fsdp', 'rep')
Inputs may be any that keep to these rules, and one draw needn't show every extreme that they name: `lengths`: in each group of 2 consecutive rows, one row, drawn from the seed, has all 1024 slots used. The 6 routes of a token name different experts. Within each aligned block of 64 positions of a row, no expert is named by more than 36 routes.
All inputs are finite; a program needn't handle non-finite values.
Results may differ from a plain program's by a relative error of at most 0.028.
Values may be sent and summed in bfloat16 or wider, within the bound.
No kernel may reach another device: no remote copies, remote signals or barrier semaphores. Data moves between devices by JAX's collectives and lax.ppermute only.
A program may use at most 512 MiB of HBM per device.

v0:
```python
import functools

import jax
import jax.numpy as jnp
from jax import lax
from jax.experimental import pallas as pl
from jax.experimental.pallas import tpu as pltpu
from jax.sharding import PartitionSpec as P

H = 16
DN = 128
DR = 64
DV = 128
R = 512
TOP = 6
MICRO = 2

EPS = 1e-06
THETA = 10000.0
F32 = jnp.float32
BF16 = jnp.bfloat16


def contract(form, left, right):
    return jnp.einsum(form, left, right, preferred_element_type=F32)


def rms_forward(value, gain):
    factor = lax.rsqrt(jnp.mean(value * value, axis=-1, keepdims=True) + EPS)
    return (value * factor * gain, factor)


def rms_backward(value, factor, gain, grad):
    scaled = grad * gain
    inner = jnp.mean(value * scaled, axis=-1, keepdims=True)
    return (
        factor * scaled - value * factor * factor * factor * inner,
        jnp.sum(grad * value * factor, axis=0),
    )


def rotate_back(grad, cosine, sine):
    half = grad.shape[-1] // 2
    first = grad[..., :half]
    second = grad[..., half:]
    return jnp.concatenate(
        [first * cosine + second * sine, second * cosine - first * sine], axis=-1
    )


def swapped(weight):
    half = weight.shape[1] // 2
    return [-weight[:, half:], weight[:, :half]]


def named(function):
    def scoped(name, *args):
        with jax.named_scope(name):
            return function(*args)

    return scoped


def near_first(outer):
    return [0] + [k for _, k in sorted((min(k, outer - k), k) for k in range(1, outer))]


def partners(devices, q, k):
    outer = devices // 4
    return [(d, ((d // 4 + k) % outer) * 4 + ((d % 4) ^ q)) for d in range(devices)]


def pull(value, devices, q, k=0):
    perm = [(there, here) for here, there in partners(devices, q, k)]
    return lax.ppermute(value, "fsdp", perm)


def push(value, devices, q, k=0):
    return lax.ppermute(value, "fsdp", partners(devices, q, k))


def order_after(values, marks):
    values, marks = list(values), list(marks)
    if not marks:
        return values, marks
    both = lax.optimization_barrier(tuple(values + marks))
    return list(both[: len(values)]), list(both[len(values) :])


def total(first, *others):
    value = first.astype(F32)
    for item in others:
        value = value + item.astype(F32)
    return value


@named
def gather_small(block, devices, cross_marks=(), last_marks=()):
    outer = devices // 4
    half = outer // 2
    base = jnp.stack([block] + [pull(block, devices, 0, k) for k in near_first(outer)[1:]])
    (sent,), cross_marks = order_after([base], cross_marks)
    one = pull(sent, devices, 1)
    two = pull(sent, devices, 2)
    (low, high), last_marks = order_after([one[:half], two[half:]], last_marks)
    low, high = pull(low, devices, 2), pull(high, devices, 1)
    return [base, one, two, low, high], cross_marks, last_marks


@named
def scatter_small_last(pieces, devices):
    base, one, two, low, high = pieces
    half = devices // 8
    low = push(low, devices, 2)
    high = push(high, devices, 1)
    zero = (0,) * one.ndim
    one = lax.dynamic_update_slice(one, total(one[:half], low).astype(BF16), zero)
    two = lax.dynamic_update_slice(
        two, total(two[half:], high).astype(BF16), (half,) + zero[1:]
    )
    return base, one, two


@named
def scatter_small_rest(pieces, devices, marks=()):
    base, one, two = pieces
    outer = devices // 4
    base = total(base, push(one, devices, 1), push(two, devices, 2))
    (sent,), marks = order_after([base[1:].astype(BF16)], marks)
    order = near_first(outer)
    return total(
        base[0], *[push(sent[i - 1], devices, 0, order[i]) for i in range(1, outer)]
    ), marks


@named
def gather_tree(block, devices, marks):
    outer = devices // 4
    half, part = outer // 2, outer // 4
    marks = [list(items) for items in marks]
    held = [block]
    for k in near_first(outer)[1:]:
        held.append(pull(block, devices, 0, k))
    pieces = [[], [], [], []]
    before = []
    for place, base in enumerate((held[:half], held[half:])):
        base = jnp.stack(base)
        if place == 0:
            (base,), marks[0] = order_after([base], marks[0])
        else:
            (base,), given = order_after([base], before + marks[1])
            pieces[1], pieces[2], marks[1] = given[0:1], given[1:2], given[2:]
        one = pull(base, devices, 1)
        two = pull(base, devices, 2)
        before = [one, two]
        low, high = one[:part], two[part:]
        if place:
            (low, high), given = order_after([low, high], pieces[3] + marks[2])
            pieces[3], marks[2] = given[:2], given[2:]
        last = [pull(low, devices, 2), pull(high, devices, 1)]
        for q, items in enumerate(([base], [one], [two], last)):
            pieces[q] += items
    return sum(pieces, []), marks


@named
def scatter_tree_last(pieces, devices):
    part = devices // 16
    halves = []
    for here in (1, 0):
        base, one, two = pieces[here], pieces[2 + here], pieces[4 + here]
        low, high = pieces[6 + 2 * here : 8 + 2 * here]
        low = push(low, devices, 2)
        high = push(high, devices, 1)
        zero = (0,) * one.ndim
        one = lax.dynamic_update_slice(one, total(one[:part], low).astype(BF16), zero)
        two = lax.dynamic_update_slice(
            two, total(two[part:], high).astype(BF16), (part,) + zero[1:]
        )
        halves.append((base, one, two))
    return halves


@named
def scatter_tree_cross(halves, devices):
    bases = []
    for base, one, two in halves:
        one = push(one, devices, 1)
        two = push(two, devices, 2)
        bases.append([total(base[i], one[i], two[i]) for i in range(base.shape[0])])
    return bases


@named
def scatter_tree_rest(bases, devices, marks=()):
    outer = devices // 4
    order = near_first(outer)
    sent, marks = order_after(
        [item.astype(BF16) for item in bases[0] + bases[1][1:]], marks
    )
    steps = order[outer // 2 :] + order[1 : outer // 2]
    arrived = [push(item, devices, 0, k) for item, k in zip(sent, steps)]
    return total(bases[1][0], *arrived), marks


def order_bases(bases, marks):
    values, marks = order_after(bases[0] + bases[1], marks)
    half = len(bases[0])
    return [values[:half], values[half:]], marks


def tree_sizes(devices):
    outer = devices // 4
    return [outer // 2] * 6 + [outer // 4] * 4


def small_split(value):
    count = value.shape[0] // 4
    half = count // 2
    cuts = (0, count, 2 * count, 3 * count, 3 * count + half, 4 * count)
    return [value[a:b] for a, b in zip(cuts, cuts[1:])]


LIMIT = 58 * 1024 * 1024


def mm(left, right):
    return jnp.dot(left, right, preferred_element_type=F32)


def mm_t(left, right):
    return lax.dot_general(left, right, (((1,), (1,)), ((), ())), preferred_element_type=F32)


def t_mm(left, right):
    return lax.dot_general(left, right, (((0,), (0,)), ((), ())), preferred_element_type=F32)


TREE = 10


def call(kernel, out_shape, places, scratch, flops, moved, *args, outs=None, aliases=None, marks=()):
    count = len(args)

    def without_marks(*refs):
        kernel(*refs[:count], *refs[count + len(marks) :])

    outs = outs or [pltpu.VMEM] * len(out_shape)
    places = list(places) + [pl.ANY] * len(marks)
    return pl.pallas_call(
        without_marks,
        out_shape=out_shape,
        in_specs=[pl.BlockSpec(memory_space=place) for place in places],
        out_specs=tuple(pl.BlockSpec(memory_space=place) for place in outs),
        input_output_aliases=aliases or {},
        scratch_shapes=scratch,
        compiler_params=pltpu.CompilerParams(vmem_limit_bytes=LIMIT),
        cost_estimate=pl.CostEstimate(flops=flops, bytes_accessed=moved, transcendentals=0),
    )(*args, *marks)


def sds(shape, dtype=BF16):
    return jax.ShapeDtypeStruct(shape, dtype)


def tree_copies(pieces, whole, sems, m, out=False):
    tok = whole.shape[1]
    copies, at = [], 0
    for place, piece in enumerate(pieces):
        count = piece.shape[0]
        ends = piece.at[:, pl.ds(m * tok, tok)], whole.at[pl.ds(at, count)]
        if out:
            ends = ends[::-1]
        copies.append(pltpu.make_async_copy(*ends, sems.at[place]))
        at += count
    return copies


def run(copies):
    for copy in copies:
        copy.start()
    for copy in copies:
        copy.wait()


def rows_of(whole, start, count):
    value = whole[pl.ds(start, count)]
    return value.reshape(count * value.shape[1], value.shape[2])


def attend_kernel(
    order, length, *refs,
):
    pieces = refs[:TREE]
    (query_w, latent_w, expand_w, gain, latent_gain, turn, pos_q, pos_k,
     out, q_nope, q_rot, k_nope, k_rot, val, latent_n, probs, factor, latent_own,
     x, sems) = refs[TREE:]
    blocks, tok, width = x.shape
    quarter = blocks // 4
    span = quarter * tok
    scale = (DN + DR) ** (-0.5)
    lane = lax.broadcasted_iota(jnp.int32, (1, 128), 1)
    loads = [tree_copies(pieces, x, sems, m) for m in range(MICRO)]
    for copy in loads[0]:
        copy.start()
    for m in range(MICRO):
        for copy in loads[m]:
            copy.wait()

        @pl.loop(0, 4)
        def _(g):
            here = pl.ds(pl.multiple_of(g * span, span), span)
            value = rows_of(x, g * quarter, quarter).astype(F32)
            inv = lax.rsqrt(jnp.mean(value * value, axis=-1, keepdims=True) + EPS)
            factor[m, here, :] = inv
            normed = (value * inv * gain[...]).astype(BF16)
            query = mm(normed, query_w[...])
            mixed = mm(normed, latent_w[...])
            latent = mixed[:, :R]

            @pl.when(g == 0)
            def _():
                latent_own[m] = latent[:tok]

            inv_l = lax.rsqrt(jnp.mean(latent * latent, axis=-1, keepdims=True) + EPS)
            low = (latent * inv_l * latent_gain[...]).astype(BF16)
            latent_n[m, here, :] = low
            q_nope[m, here, :] = query[:, :DN].astype(BF16)
            turned = query[:, DN:] * turn[here, :]
            q_rot[m, here, :] = (turned + pltpu.roll(turned, DR, 1)).astype(BF16)
            turned = mixed[:, R:] * turn[here, :]
            k_rot[m, here, :] = (turned + pltpu.roll(turned, DR, 1)).astype(BF16)
            kv = mm(low, expand_w[...])
            k_nope[m, here, :] = kv[:, :DN].astype(BF16)
            val[m, here, :] = kv[:, DN:].astype(BF16)

        if m + 1 < MICRO:
            for copy in loads[m + 1]:
                copy.start()
        half_k = jnp.where(lane < DR, k_rot[m], jnp.zeros_like(k_rot[m]))

        @pl.loop(0, 4)
        def _(g):
            here = pl.ds(pl.multiple_of(g * span, span), span)
            scores = mm_t(q_nope[m, here, :], k_nope[m]) + mm_t(q_rot[m, here, :], half_k)
            visible = (pos_k[...] <= pos_q[here, :]) & (pos_k[...] < length[m])
            scores = jnp.where(visible, scores * scale, -1e30)
            raised = jnp.exp(scores - jnp.max(scores, axis=-1, keepdims=True))
            prob = (raised / jnp.sum(raised, axis=-1, keepdims=True)).astype(BF16)
            probs[m, here, :] = prob
            value = mm(prob, val[m]).astype(BF16).reshape(quarter, tok, DV)
            for i in range(quarter):
                out[order[g * quarter + i], pl.ds(m * tok, tok), :] = value[i]


def attend(order, length, pieces, query_w, latent_w, expand_w, gain, latent_gain, turn, pos):
    blocks = sum(piece.shape[0] for piece in pieces)
    tok, width = pieces[0].shape[1] // MICRO, query_w.shape[0]
    seq = blocks * tok
    small = sds((MICRO, seq, 128))
    return call(
        attend_kernel,
        (sds((blocks, MICRO * tok, DV)), small, small, small, small, small,
         sds((MICRO, seq, R)), sds((MICRO, seq, seq)), sds((MICRO, seq, 1), F32),
         sds((MICRO, tok, R), F32)),
        [pltpu.SMEM] * 2 + [pl.ANY] * TREE + [pltpu.VMEM] * 8,
        [pltpu.VMEM((blocks, tok, width), BF16), pltpu.SemaphoreType.DMA((TREE,))],
        2 * MICRO * seq * (width * 896 + R * 256 + seq * 384),
        2 * MICRO * seq * (width + seq + 1200) + 1800 * width,
        order, length, *pieces, query_w, latent_w, expand_w, gain.reshape(1, -1),
        latent_gain.reshape(1, -1), turn, pos.reshape(seq, 1), pos.reshape(1, seq),
    )


def attend_back_kernel(order, *refs):
    pieces = refs[:TREE]
    (grad, q_nope, q_rot, k_nope, k_rot, val, latent_n, probs, factor, query_w, expand_w, gain,
     turn) = refs[TREE : TREE + 13]
    (grad_queries, l0, l1, l2, l3, l4, grad_query_w, grad_expand_w, part,
     x, prob_all, grad_k, grad_r, grad_v, sems, prob_sem) = refs[TREE + 13 :]
    blocks, tok, width = x.shape
    quarter = blocks // 4
    span = quarter * tok
    scale = (DN + DR) ** (-0.5)
    grad_query_w[...] = jnp.zeros_like(grad_query_w)
    part[...] = jnp.zeros_like(part)
    lane = lax.broadcasted_iota(jnp.int32, (1, 128), 1)
    for m in range(MICRO):
        load = pltpu.make_async_copy(probs.at[m], prob_all, prob_sem)
        run(tree_copies(pieces, x, sems, m) + [load])
        grad_k[...] = jnp.zeros_like(grad_k)
        grad_r[...] = jnp.zeros_like(grad_r)
        grad_v[...] = jnp.zeros_like(grad_v)

        @pl.loop(0, 4)
        def _(g):
            here = pl.ds(pl.multiple_of(g * span, span), span)
            above = jnp.concatenate(
                [grad[order[g * quarter + i], pl.ds(m * tok, tok), :] for i in range(quarter)],
                axis=0,
            )
            prob_low = prob_all[here, :]
            prob = prob_low.astype(F32)
            weighted = prob * mm_t(above, val[m])
            slope = (weighted - prob * jnp.sum(weighted, axis=-1, keepdims=True)).astype(BF16)
            grad_k[...] += t_mm(slope, q_nope[m, here, :])
            grad_r[...] += t_mm(slope, q_rot[m, here, :])
            grad_v[...] += t_mm(prob_low, above)
            nope = (mm(slope, k_nope[m]) * scale).astype(BF16)
            turned = mm(slope, k_rot[m]) * (scale * turn[here, :])
            grad_q = jnp.concatenate([nope, turned.astype(BF16)], axis=1)
            back = jnp.where(
                lane < DR // 2,
                turned + pltpu.roll(turned, DR // 2, 1),
                turned - pltpu.roll(turned, 128 - DR // 2, 1),
            )
            both = jnp.concatenate([nope, back.astype(BF16)], axis=1).reshape(quarter, tok, 256)
            for i in range(quarter):
                grad_queries[order[g * quarter + i], pl.ds(m * tok, tok), :] = both[i]
            value = rows_of(x, g * quarter, quarter).astype(F32) * factor[m, here, :]
            grad_query_w[...] += t_mm((value * gain[...]).astype(BF16), grad_q)
            normed = mm_t(grad_q, query_w[...])
            part[...] += jnp.sum(normed * value, axis=0, keepdims=True)

        grad_kv = jnp.concatenate([grad_k[...] * scale, grad_v[...]], axis=1).astype(BF16)
        expand_sum = t_mm(latent_n[m], grad_kv)
        grad_expand_w[...] = expand_sum if m == 0 else grad_expand_w[...] + expand_sum
        latent = jnp.concatenate(
            [mm_t(grad_kv, expand_w[...]).astype(BF16), (grad_r[...] * scale).astype(BF16)], axis=1
        ).reshape(blocks, tok, R + 128)
        at = 0
        for ref in (l0, l1, l2, l3, l4):
            count = ref.shape[0]
            ref[:, pl.ds(m * tok, tok), :] = latent[at : at + count]
            at += count


def attend_back(order, pieces, grad, saved, query_w, expand_w, gain, turn, marks):
    blocks = sum(piece.shape[0] for piece in pieces)
    both, width = pieces[0].shape[1], query_w.shape[0]
    tok = both // MICRO
    seq = blocks * tok
    quarter = blocks // 4
    sizes = (quarter,) * 3 + (quarter // 2,) * 2
    return call(
        attend_back_kernel,
        (sds((blocks, both, 256)),)
        + tuple(sds((count, both, R + 128)) for count in sizes)
        + (sds((width, 256), F32), sds((R, 256), F32), sds((1, width), F32)),
        [pltpu.SMEM] + [pl.ANY] * TREE + [pltpu.VMEM] * 7 + [pl.ANY] + [pltpu.VMEM] * 5,
        [pltpu.VMEM((blocks, tok, width), BF16), pltpu.VMEM((seq, seq), BF16)]
        + [pltpu.VMEM((seq, 128), F32)] * 3
        + [pltpu.SemaphoreType.DMA((TREE,)), pltpu.SemaphoreType.DMA],
        2 * MICRO * seq * (width * 512 + R * 512 + seq * 768),
        2 * MICRO * seq * (2 * width + seq + 2000) + 2 * query_w.size,
        order, *pieces, grad, *saved[1:9], query_w, expand_w, gain.reshape(1, -1), turn,
        marks=marks,
    )


def early_kernel(m, *refs):
    pieces = refs[:TREE]
    pick, row_gate, down, shared_down, back, grad_eh, grad_shared, whole, g, sems = refs[TREE:]
    blocks, tok, width = g.shape
    quarter = blocks // 4
    room = pick.shape[1]
    run(tree_copies(pieces, g, sems, m))

    @pl.loop(0, 4)
    def _(q):
        value = rows_of(g, q * quarter, quarter)
        here = pl.ds(pl.multiple_of(q * room, room), room)
        back[here, :] = (row_gate[here, :] * mm(pick[q], value)).astype(BF16)
        span = quarter * tok
        there = pl.ds(pl.multiple_of(q * span, span), span)
        grad_shared[there, :] = mm_t(value, shared_down[...])
        whole[there, :] = value

    chunks = down.shape[0] // 128

    @pl.loop(0, chunks)
    def _(f):
        here = pl.ds(pl.multiple_of(f * 128, 128), 128)
        grad_eh[:, here] = mm_t(back[...], down[here, :])


def early(m, pieces, pick, row_gate, down, shared_down, marks):
    blocks = sum(piece.shape[0] for piece in pieces)
    tok, width = pieces[0].shape[1] // MICRO, down.shape[1]
    rows, units = pick.shape[0] * pick.shape[1], shared_down.shape[0]
    return call(
        functools.partial(early_kernel, m),
        (sds((rows, width)), sds((rows, down.shape[0]), F32), sds((blocks * tok, units), F32),
         sds((blocks * tok, width))),
        [pl.ANY] * TREE + [pltpu.VMEM] * 4,
        [pltpu.VMEM((blocks, tok, width), BF16), pltpu.SemaphoreType.DMA((TREE,))],
        2 * rows * width * (down.shape[0] + 256),
        2 * width * (2 * blocks * tok + rows + down.shape[0]) + 4 * rows * down.shape[0],
        *pieces, pick, row_gate, down, shared_down, marks=marks,
    )


def expert_kernel(m, *refs):
    pieces = refs[:TREE]
    pick, grad_eh, grad_shared, both, share_g, share_u = refs[TREE : TREE + 6]
    first = TREE + 6 + (TREE if m else 0)
    mixed, arrived, hidden, grad_gu, shared_hidden, grad_sg, grad_su = refs[first : first + 7]
    outs = refs[first + 7 : first + 7 + TREE]
    x, w, o, sems, w_sems = refs[first + 7 + TREE :]
    blocks, tok, width = x.shape
    quarter = blocks // 4
    span = quarter * tok
    room = pick.shape[1]
    chunks = w.shape[0] // 256
    copies = tree_copies(pieces, x, sems, m)
    for copy in copies:
        copy.start()
    loads = [
        pltpu.make_async_copy(both.at[pl.ds(f * 256, 256)], w.at[pl.ds(f * 256, 256)], w_sems.at[f])
        for f in range(chunks)
    ]
    for copy in loads:
        copy.start()
    for copy in copies:
        copy.wait()

    @pl.loop(0, 4)
    def _(q):
        value = rows_of(x, q * quarter, quarter)
        there = pl.ds(pl.multiple_of(q * span, span), span)
        here = pl.ds(pl.multiple_of(q * room, room), room)
        mixed[there, :] = value
        arrived[here, :] = mm(pick[q], value).astype(BF16)
        gate = mm(value, share_g[...])
        lift = mm(value, share_u[...])
        sigma = 1.0 / (1.0 + jnp.exp(-gate))
        grad = grad_shared[there, :]
        shared_hidden[there, :] = (gate * sigma * lift).astype(BF16)
        grad_sg[there, :] = (grad * lift * sigma * (1.0 + gate * (1.0 - sigma))).astype(BF16)
        grad_su[there, :] = (grad * gate * sigma).astype(BF16)

    for copy in loads:
        copy.wait()

    @pl.loop(0, chunks)
    def _(f):
        rows = pl.ds(pl.multiple_of(f * 256, 256), 256)
        cols = pl.ds(pl.multiple_of(f * 128, 128), 128)
        value = mm_t(arrived[...], w[rows, :])
        gate, lift = value[:, :128], value[:, 128:]
        sigma = 1.0 / (1.0 + jnp.exp(-gate))
        grad = grad_eh[:, cols]
        hidden[:, cols] = (gate * sigma * lift).astype(BF16)
        grad_gu[:, rows] = jnp.concatenate(
            [
                (grad * lift * sigma * (1.0 + gate * (1.0 - sigma))).astype(BF16),
                (grad * gate * sigma).astype(BF16),
            ],
            axis=1,
        )

    spread_out(
        o, pick, 512,
        lambda cols: mm(grad_gu[...], w[:, cols]).astype(BF16),
        lambda there, cols: mm_t(grad_sg[there, :], share_g[cols, :])
        + mm_t(grad_su[there, :], share_u[cols, :]),
    )
    run(tree_copies(outs, o, sems, m, True))


def spread_out(o, pick, step, routed, shared):
    blocks, tok, width = o.shape
    quarter = blocks // 4
    span = quarter * tok
    room = pick.shape[1]

    @pl.loop(0, width // step)
    def _(c):
        cols = pl.ds(pl.multiple_of(c * step, step), step)
        value = routed(cols)
        for q in range(4):
            there = pl.ds(q * span, span)
            tokens = t_mm(pick[q], value[q * room : (q + 1) * room]) + shared(there, cols)
            o[pl.ds(q * quarter, quarter), :, cols] = tokens.astype(BF16).reshape(
                quarter, tok, step
            )


def experts(m, pieces, pick, grad_eh, grad_shared, both, share_g, share_u, earlier):
    blocks = sum(piece.shape[0] for piece in pieces)
    tok, width = pieces[0].shape[1] // MICRO, pieces[0].shape[2]
    seq, rows, units = blocks * tok, pick.shape[0] * pick.shape[1], share_g.shape[1]
    hid = both.shape[0] // 2
    whole = pltpu.VMEM((blocks, tok, width), BF16)
    return call(
        functools.partial(expert_kernel, m),
        (sds((seq, width)), sds((rows, width)), sds((rows, hid)), sds((rows, 2 * hid)))
        + (sds((seq, units)),) * 3 + tuple(sds(piece.shape) for piece in pieces),
        [pl.ANY] * TREE + [pltpu.VMEM] * 3 + [pl.ANY] + [pltpu.VMEM] * 2
        + [pl.ANY] * len(earlier),
        [whole, pltpu.VMEM(both.shape, BF16), whole,
         pltpu.SemaphoreType.DMA((TREE,)), pltpu.SemaphoreType.DMA((both.shape[0] // 256,))],
        8 * rows * width * hid + 8 * seq * width * 256,
        2 * both.size + 6 * seq * width + 10 * rows * hid,
        *pieces, pick, grad_eh, grad_shared, both, share_g, share_u, *earlier,
        outs=[pltpu.VMEM] * 7 + [pl.ANY] * TREE,
        aliases={TREE + 6 + i: 7 + i for i in range(len(earlier))},
    )


def output_kernel(m, *refs):
    hidden, row_gate, pick, down, shared_hidden, shared_down = refs[:6]
    first = 6 + (TREE if m else 0)
    outs = refs[first : first + TREE]
    o, sems = refs[first + TREE :]
    spread_out(
        o, pick, 512,
        lambda cols: (
            row_gate[...] * mm(hidden[...], down[:, cols]).astype(BF16).astype(F32)
        ).astype(BF16),
        lambda there, cols: mm(shared_hidden[there, :], shared_down[:, cols]),
    )
    run(tree_copies(outs, o, sems, m, True))


def expert_output(m, pieces, hidden, row_gate, pick, down, shared_hidden, shared_down, earlier,
                  marks):
    blocks = sum(piece.shape[0] for piece in pieces)
    tok, width = pieces[0].shape[1] // MICRO, pieces[0].shape[2]
    return call(
        functools.partial(output_kernel, m),
        tuple(sds(piece.shape) for piece in pieces),
        [pltpu.VMEM] * 6 + [pl.ANY] * len(earlier),
        [pltpu.VMEM((blocks, tok, width), BF16), pltpu.SemaphoreType.DMA((TREE,))],
        2 * hidden.size * width + 4 * blocks * tok * 256 * width,
        2 * down.size + 2 * hidden.size + 2 * blocks * tok * width,
        hidden, row_gate, pick, down, shared_hidden, shared_down, *earlier,
        marks=marks,
        outs=[pl.ANY] * TREE,
        aliases={6 + i: i for i in range(len(earlier))},
    )


def weight_kernel(reps, count, *refs):
    l0, l1, r0, r1, *outs = refs[count:]
    unit = 128 // reps
    value = t_mm(l0[...], r0[...]) + t_mm(l1[...], r1[...])
    for index, ref in enumerate(outs):
        for part in range(reps):
            start = index * 128 + part * unit
            ref[part] = value[start : start + unit].astype(ref.dtype)


def weight_sums(reps, lanes, left, right, marks):
    rows, width = right[0].shape
    hid = left[0].shape[1] * 128 // lanes
    chunks, unit = hid // 128, 128 // reps
    whole = pl.BlockSpec((rows, width), lambda f: (0, 0), pipeline_mode=pl.Buffered(1))
    part = pl.BlockSpec((reps, unit, width), lambda f: (0, f, 0))
    return pl.pallas_call(
        functools.partial(weight_kernel, reps, len(marks)),
        grid=(chunks,),
        in_specs=[pl.BlockSpec(memory_space=pl.ANY)] * len(marks)
        + [pl.BlockSpec((rows, lanes), lambda f: (0, f))] * 2 + [whole] * 2,
        out_specs=[part] * (lanes // 128),
        out_shape=[sds((reps, hid // reps, width))] * (lanes // 128),
        compiler_params=pltpu.CompilerParams(vmem_limit_bytes=LIMIT),
        cost_estimate=pl.CostEstimate(
            flops=4 * rows * width * hid * lanes // 128,
            bytes_accessed=10 * width * hid,
            transcendentals=0,
        ),
    )(*marks, *left, *right)


def rep_pull(value, count, step):
    return lax.ppermute(value, "rep", [((d + step) % count, d) for d in range(count)])


def rep_parts(value, count):
    return [value] + [rep_pull(value, count, step) for step in range(1, count)]


def rep_total(parts, count):
    value = parts[0].astype(F32)
    for step in range(1, count):
        perm = [(d, (d + step) % count) for d in range(count)]
        value = value + lax.ppermute(parts[step], "rep", perm).astype(F32)
    return value


def rep_sum(value):
    return jnp.sum(lax.all_gather(value.astype(BF16), "rep", axis=0).astype(F32), axis=0)


def body(
    hidden_in,
    cotangent,
    lengths,
    routes,
    gate_values,
    attn_gain,
    query_proj,
    latent_proj,
    latent_gain,
    expand_proj,
    output_proj,
    ffn_gain,
    shared_gate,
    shared_lift,
    shared_down,
    expert_gate,
    expert_lift,
    expert_down,
):
    tok = hidden_in.shape[1]
    width = hidden_in.shape[2]
    n = lax.axis_size("fsdp")
    reps = lax.axis_size("rep")
    me = lax.axis_index("fsdp")
    rep = lax.axis_index("rep")
    outer = n // 4
    seq = tok * n
    capacity = min(tok, 3 * tok * TOP // (2 * n))
    split = max(1, n // H)
    rows = width // n

    slots = jnp.arange(n, dtype=jnp.int32)
    nearness = near_first(outer)
    steps_on = jnp.asarray(nearness, jnp.int32)
    place_of = jnp.asarray([nearness.index(k) for k in range(outer)], jnp.int32)
    abs_of_rel = ((me // 4 + steps_on[slots % outer]) % outer) * 4 + ((me % 4) ^ (slots // outer))
    rel_of_abs = ((slots % 4) ^ (me % 4)) * outer + place_of[(slots // 4 - me // 4) % outer]
    rep_order = (jnp.arange(reps, dtype=jnp.int32) - rep) % reps
    own_pos = me * tok + jnp.arange(tok, dtype=jnp.int32)
    pos = (abs_of_rel[:, None] * tok + jnp.arange(tok, dtype=jnp.int32)[None, :]).reshape(seq)
    freqs = THETA ** (-(2.0 * jnp.arange(DR // 2, dtype=F32)) / DR)
    angles = pos.astype(F32)[:, None] * freqs[None, :]
    cosine, sine = jnp.cos(angles), jnp.sin(angles)
    turn = jnp.concatenate([cosine, cosine, sine, sine], axis=1)

    def all_to_all(value):
        return lax.all_to_all(value, "fsdp", split_axis=0, concat_axis=0, tiled=True)

    def rep_slice(value, axis):
        size = value.shape[axis] // reps
        return lax.dynamic_slice_in_dim(value, rep * size, size, axis)

    def rep_join(value, axis):
        parts = jnp.take(jnp.stack(rep_parts(value, reps)), rep_order, axis=0)
        return jnp.concatenate([parts[i] for i in range(reps)], axis=axis)

    def unreshard(value):
        return rep_sum(all_to_all(value.astype(BF16)))

    def by_head(value):
        return jnp.repeat(value, split, axis=0) if split > 1 else value

    both = MICRO * tok
    dense_gate = jnp.sum(
        jnp.where(routes[..., None] == slots, gate_values[..., None], 0.0), axis=2
    ).reshape(both, n)
    gate_high = dense_gate.astype(BF16)
    gate_low = (dense_gate - gate_high.astype(F32)).astype(BF16)

    def fit(value):
        return jnp.pad(value, ((0, both - value.shape[0]), (0, 0)))

    items = [
        fit(latent_proj),
        gate_high,
        gate_low,
        fit(attn_gain[:, None]),
        fit(ffn_gain[:, None]),
        fit(latent_gain[:, None]),
    ]
    starts = [0]
    for item in items:
        starts.append(starts[-1] + item.shape[1])
    fill = jnp.zeros((both, -starts[-1] % 128), BF16)
    small = gather_small("small", jnp.concatenate(items + [fill], axis=1), n)[0]
    extras = jnp.concatenate(small, axis=0)
    latent_w = jnp.take(extras[:, :rows, : starts[1]], rel_of_abs, axis=0).reshape(width, R + DR)
    gates = extras[..., starts[1] : starts[3]].reshape(n, both, 2, n).astype(F32)
    gates = jnp.sum(jnp.where(slots == me, gates, 0.0), axis=(2, 3))
    gains = jnp.take(extras[..., starts[3] : starts[6]], rel_of_abs, axis=0).astype(F32)
    gains = jnp.transpose(gains, (2, 0, 1))
    attn_gain_f = gains[0, :, :rows].reshape(width)
    ffn_gain_f = gains[1, :, :rows].reshape(width)
    latent_gain_f = gains[2, :, : R // n].reshape(R)

    head_w = jnp.concatenate(
        [
            jnp.transpose(query_proj.reshape(rows, H, DN + DR), (1, 0, 2)),
            jnp.transpose(expand_proj.reshape(R // n, H, DN + DV), (1, 0, 2)).reshape(
                H, rows, -1
            ),
        ],
        axis=2,
    )
    head_w = all_to_all(by_head(head_w))
    query_w = head_w[..., : DN + DR].reshape(width, DN + DR)
    expand_w = head_w[..., DN + DR :].reshape(R, DN + DV)
    query_w = jnp.concatenate([query_w] + swapped(query_w[:, DN:]), axis=1)
    latent_in = jnp.concatenate([latent_w] + swapped(latent_w[:, R:]), axis=1)

    unit = 128 // reps

    def chunked(*weights):
        parts = [lax.all_gather(item, "rep", axis=0) for item in weights]
        return jnp.stack(
            [part[i].reshape(-1, unit, width) for part in parts for i in range(reps)], axis=1
        ).reshape(-1, width)

    both_w = chunked(jnp.swapaxes(expert_gate[0], 0, 1), jnp.swapaxes(expert_lift[0], 0, 1))
    down_w = chunked(expert_down[0])
    block = hidden_in.reshape(both, width)
    hidden_all, given = gather_tree(
        "hidden", block, n, ((), (), [query_w, latent_in, expand_w, both_w, down_w])
    )
    query_w, latent_in, expand_w, both_w, down_w = given[2]

    cols = width // reps
    used = (own_pos[None, :] < lengths[:, None])[..., None]
    grad_rows = jnp.where(used, cotangent, jnp.zeros_like(cotangent)).reshape(both, width)
    (out_share,), hidden_all[1:2] = order_after([rep_slice(output_proj, 1)], hidden_all[1:2])
    out_marks = hidden_all[3:4]
    att = attend(
        abs_of_rel, lengths, hidden_all, query_w, latent_in, expand_w,
        attn_gain_f, latent_gain_f, turn, pos,
    )
    att = list(att)

    out_pieces, _, att[0:1] = gather_small("output_w", out_share, n, out_marks, att[0:1])
    heads_out = all_to_all(att[0])
    (grad_rows,), out_pieces[0:1] = order_after([grad_rows], out_pieces[0:1])
    grad_all, given = gather_tree("cotangent", grad_rows, n, (out_pieces[1:3] + [heads_out], (), ()))
    out_pieces[1], out_pieces[2], heads_out = given[0]
    heads_out = heads_out[::split]
    heads_local = jnp.transpose(heads_out, (1, 0, 2)).reshape(both, n, H * DV // n)
    heads_local = jnp.take(heads_local, abs_of_rel, axis=1).reshape(both, H * DV)
    cols = width // reps
    out_w = rep_parts(jnp.concatenate(out_pieces, axis=0).reshape(H * DV, cols), reps)

    def columns(step):
        return ((rep + step) % reps) * cols

    merge = 1
    while (merge * capacity) % 16:
        merge *= 2
    groups = n // merge
    span = merge * tok
    room = merge * capacity
    upper = (jnp.arange(span)[:, None] <= jnp.arange(span)[None, :]).astype(BF16)

    hidden = hidden_in.reshape(both, width).astype(F32)
    residual = jnp.zeros((both, width), F32)
    for step in range(reps):
        share = contract("tj,jd->td", heads_local, out_w[step])
        residual = lax.dynamic_update_slice(residual, share, (0, columns(step)))
    residual = hidden + residual
    mixed, inv_second = rms_forward(residual, ffn_gain_f)
    mixed = mixed.astype(BF16)
    (shared_gate, shared_lift), (mixed,) = order_after([shared_gate, shared_lift], [mixed])

    ahead = []
    for m in range(MICRO):
        gate_here = gates[:, m * tok : (m + 1) * tok].reshape(groups, span)
        hit = gate_here > 0.0
        place = contract("gt,ts->gs", hit.astype(BF16), upper).astype(jnp.int32) - 1
        chosen = hit[:, None, :] & (
            place[:, None, :] == jnp.arange(room, dtype=jnp.int32)[None, :, None]
        )
        pick = chosen.astype(BF16)
        row_gate = jnp.sum(jnp.where(chosen, gate_here[:, None, :], 0.0), axis=2).reshape(-1, 1)
        ahead.append(
            (pick, row_gate) + early(m, grad_all, pick, row_gate, down_w, shared_down,
                    (ahead[0][2],) if m else (mixed,))
        )

    shared_in = jnp.concatenate(
        [
            jnp.transpose(shared_gate.reshape(rows, n, -1), (1, 0, 2)),
            jnp.transpose(shared_lift.reshape(rows, n, -1), (1, 0, 2)),
        ],
        axis=2,
    )
    units = shared_in.shape[2] // 2
    shared_in = all_to_all(shared_in)
    marks = [list(item) for item in ahead]
    mixed_all, given = gather_tree(
        "mixed", mixed, n, ((), [marks[0][2], shared_in, both_w], [marks[1][2]])
    )
    marks[0][2], shared_in, both_w = given[1]
    marks[1][2:3] = given[2]
    shared_in = shared_in.reshape(width, 2 * units)
    ahead = marks

    share_g, share_u = shared_in[:, :units], shared_in[:, units:]

    share = jnp.concatenate([rep_slice(query_proj, 1)], axis=1)
    (share,), mixed_all[8:] = order_after([share], mixed_all[8:])
    whole_query = lax.all_gather(share, "fsdp", axis=0, tiled=True)

    done = []
    earlier = ()
    for m in range(MICRO):
        pick, row_gate, back, grad_eh, grad_shared, _ = ahead[m]
        done.append(
            experts(m, mixed_all, pick, grad_eh, grad_shared, both_w, share_g, share_u, earlier)
        )
        earlier = done[m][7:]
    earlier = list(earlier)
    pieces = ()
    halves = scatter_tree_last("grad_mixed", earlier, n)
    bases = scatter_tree_cross("grad_mixed", halves, n)
    stages = [(halves[0][1],), (halves[1][2],), (bases[0][0],), (bases[1][0],)]
    for m in range(MICRO):
        pick, row_gate = ahead[m][:2]
        pieces = list(
            expert_output(
                m, mixed_all, done[m][2], row_gate, pick, down_w, done[m][4], shared_down,
                pieces, stages[2 * m],
            )
        )
        if m == 0:
            down_sums = list(
                weight_sums(
                    reps, 128, (done[0][2], done[1][2]), (ahead[0][2], ahead[1][2]),
                    stages[1] + (pieces[0],),
                )
            )
            share_grads, down_sums[0:1] = order_after(
                [done[0][5], done[1][5]], list(down_sums[0:1])
            )
            stages[2] += (down_sums[0],)
    down_sums = list(down_sums)
    both_sums = weight_sums(
        reps, 256, (done[0][3], done[1][3]), (done[0][1], done[1][1]),
        stages[3] + (pieces[0],),
    )
    both_sums = list(both_sums)
    grad_mixed, _ = scatter_tree_rest("grad_mixed", bases, n)
    grad_shared_in = sum(
        contract("td,tf->df", done[m][0], jnp.concatenate([share_grads[m], done[m][6]], axis=1))
        for m in range(MICRO)
    )
    grad_shared_in = all_to_all(grad_shared_in.astype(BF16).reshape(n, rows, 2 * units))
    (grad_mixed,), (both_sums[0], grad_shared_in) = order_after(
        [grad_mixed], [both_sums[0], grad_shared_in]
    )
    whole_query = lax.all_gather(whole_query, "rep", axis=0)
    expert_sums = [
        lax.psum_scatter(item, "rep", scatter_dimension=0) for item in both_sums + down_sums
    ]
    grad_res, part_ffn = rms_backward(residual, inv_second, ffn_gain_f, grad_mixed)
    grad_res = grad_res + grad_rows.astype(F32)
    grad_res_low = grad_res.astype(BF16)
    grad_heads = sum(
        contract(
            "td,jd->tj",
            lax.dynamic_slice_in_dim(grad_res_low, columns(step), cols, 1),
            out_w[step],
        )
        for step in range(reps)
    )
    grad_heads = jnp.take(
        grad_heads.astype(BF16).reshape(both, n, H * DV // n), rel_of_abs, axis=1
    )
    grad_heads = jnp.transpose(grad_heads.reshape(both, H, DV), (1, 0, 2))
    grad_heads = by_head(grad_heads)
    grad_heads = all_to_all(grad_heads)
    if split > 1:
        grad_heads = jnp.where(me % split == 0, grad_heads, jnp.zeros_like(grad_heads))

    shares = []
    for step in range(reps):
        piece = lax.dynamic_slice_in_dim(grad_res_low, columns(step), cols, 1)
        shares.append(contract("tj,td->jd", heads_local, piece))
    out_total = rep_total([shares[0]] + [item.astype(BF16) for item in shares[1:]], reps)
    out_total = out_total.astype(BF16).reshape(n, rows, cols)
    out_pieces = small_split(out_total)

    result = attend_back(
        abs_of_rel, hidden_all, grad_heads, att, query_w, expand_w, attn_gain_f, turn,
        [whole_query] + expert_sums,
    )
    result = list(result)
    pieces[6:], result[6:7] = order_after(pieces[6:], result[6:7])
    halves = scatter_tree_last("routed", pieces, n)
    expert_sums, result[1:2] = order_after(expert_sums, result[1:2])
    grad_expert_gate, grad_expert_lift, grad_expert_down = [
        item.astype(F32) for item in expert_sums
    ]
    (grad_shared_in,), result[2:3] = order_after([grad_shared_in], result[2:3])
    grad_shared_in = rep_sum(grad_shared_in)
    grad_shared_gate = jnp.transpose(grad_shared_in[:, :, :units], (1, 0, 2)).reshape(rows, -1)
    grad_shared_lift = jnp.transpose(grad_shared_in[:, :, units:], (1, 0, 2)).reshape(rows, -1)
    down_sum = sum(contract("tf,td->fd", done[m][4], ahead[m][5]) for m in range(MICRO))
    grad_shared_down = rep_sum(down_sum)


    bases = scatter_tree_cross("routed", halves, n)
    grad_queries = all_to_all(result[0])
    grad_latent = scatter_small_last("grad_latent", result[1:6], n)
    grad_latent, (grad_queries,) = scatter_small_rest(
        "grad_latent", grad_latent, n, [grad_queries]
    )
    routed, (grad_latent,) = scatter_tree_rest("routed", bases, n, [grad_latent])
    outputs = (residual + routed).astype(BF16).reshape(MICRO, tok, width)
    out_pieces[3:], (grad_latent,) = order_after(out_pieces[3:], [grad_latent])
    out_pieces = scatter_small_last("grad_output_w", out_pieces, n)
    grad_q, grad_expand_w, part_attn = result[6:]

    latent = att[9].reshape(both, R)
    inv = lax.rsqrt(jnp.mean(latent * latent, axis=-1, keepdims=True) + EPS)
    grad_c, part_latent = rms_backward(latent, inv, latent_gain_f, grad_latent[:, :R])
    own_cos, own_sin = jnp.tile(cosine[:tok], (MICRO, 1)), jnp.tile(sine[:tok], (MICRO, 1))
    grad_krope = rotate_back(grad_latent[:, R : R + DR], own_cos, own_sin)
    grad_kva = jnp.concatenate([grad_c, grad_krope], axis=1).astype(BF16)
    grad_local = contract("tj,dj->td", grad_kva, latent_w)
    factor = att[8][:, :tok].reshape(both, 1)
    part_attn = part_attn[0] + jnp.sum(grad_local * hidden * factor, axis=0)

    gain_parts = jnp.stack(
        [
            part_attn.reshape(n, rows),
            part_ffn.reshape(n, rows),
            jnp.pad(part_latent.reshape(n, R // n), ((0, 0), (0, rows - R // n))),
        ],
        axis=1,
    )
    kv_pieces = gather_small("grad_kv", grad_kva, n)[0]

    turn_part = grad_q[:, DN + DR :]
    half = DR // 2
    grad_q = jnp.concatenate(
        [
            grad_q[:, :DN],
            grad_q[:, DN : DN + half] + turn_part[:, half:],
            grad_q[:, DN + half : DN + DR] - turn_part[:, :half],
        ],
        axis=1,
    )
    head_grad = jnp.concatenate(
        [grad_q.reshape(n, rows, DN + DR), grad_expand_w.reshape(n, rows, -1)], axis=2
    ).astype(BF16)
    gain_high = gain_parts.astype(BF16)
    gain_low = (gain_parts - gain_high.astype(F32)).astype(BF16)
    gain_rows = jnp.stack([gain_high, gain_low], axis=1).reshape(n, -1)
    gain_count = gain_rows.shape[1]
    head_cols = head_grad.shape[2]
    gain_rows = jnp.pad(gain_rows, ((0, 0), (0, 16 * head_cols - gain_count)))
    head_grad = jnp.concatenate([head_grad, gain_rows.reshape(n, 16, head_cols)], axis=1)
    (head_grad,), (grad_queries,) = order_after([head_grad], [grad_queries])
    head_grad = all_to_all(head_grad)
    gain_sum = head_grad[:, rows:].reshape(n, -1)[:, :gain_count].astype(F32)
    gain_sum = jnp.sum(gain_sum, axis=0).reshape(2, 3, rows)
    gain_sum = gain_sum[0] + gain_sum[1]
    head_grad = head_grad[:, :rows]
    out_sum, _ = scatter_small_rest("grad_output_w", out_pieces, n)
    (head_grad,), kv_pieces[1:2] = order_after([head_grad], kv_pieces[1:2])
    head_grad = rep_sum(head_grad)[::split]
    grad_output_proj = rep_join(out_sum.astype(BF16), 1).astype(F32)
    grad_queries = jnp.transpose(grad_queries[::split, :, : DN + DR], (1, 0, 2))
    grad_queries = grad_queries.reshape(both, reps, -1)
    grad_normed = sum(
        contract("tj,dj->td", grad_queries[:, i], whole_query[i]) for i in range(reps)
    )
    grad_first, _ = rms_backward(hidden, factor, attn_gain_f, grad_normed + grad_local)
    input_grads = (grad_first + grad_res).astype(BF16).reshape(MICRO, tok, width)

    grad_query_proj = jnp.transpose(head_grad[..., : DN + DR], (1, 0, 2)).reshape(rows, -1)
    grad_expand_proj = jnp.transpose(
        head_grad[..., DN + DR :].reshape(H, R // n, DN + DV), (1, 0, 2)
    ).reshape(R // n, H * (DN + DV))

    kv_blocks = jnp.concatenate(kv_pieces, axis=0)
    hidden_all, (grad_queries,) = order_after(hidden_all, [grad_queries])
    gain_cols = lax.dynamic_slice_in_dim(attn_gain_f, me * rows, rows, 0)
    hidden_cols = jnp.concatenate(
        [lax.dynamic_slice_in_dim(item, me * rows, rows, 2) for item in hidden_all], axis=0
    ).reshape(n, MICRO, tok, rows)
    factors = jnp.swapaxes(att[8].reshape(MICRO, n, tok, 1), 0, 1)
    normed_cols = (hidden_cols.astype(F32) * factors * gain_cols).astype(BF16)
    latent_total = contract(
        "tj,td->jd", kv_blocks.reshape(-1, R + DR), normed_cols.reshape(-1, rows)
    )
    latent_total = rep_sum(latent_total)
    grad_latent_proj = latent_total.T

    gain_sum = gain_sum + sum(rep_pull(gain_sum, reps, step) for step in range(1, reps))

    return (
        outputs,
        input_grads,
        gain_sum[0],
        grad_query_proj,
        grad_latent_proj,
        gain_sum[2, : R // n],
        grad_expand_proj,
        grad_output_proj,
        gain_sum[1],
        grad_shared_gate,
        grad_shared_lift,
        grad_shared_down,
        jnp.swapaxes(grad_expert_gate, 0, 1)[None],
        jnp.swapaxes(grad_expert_lift, 0, 1)[None],
        grad_expert_down[None],
    )


def solution(mesh):
    in_specs = (
        P("rep", "fsdp", None),
        P("rep", "fsdp", None),
        P("rep"),
        P("rep", "fsdp", None),
        P("rep", "fsdp", None),
        P("fsdp"),
        P("fsdp", None),
        P("fsdp", None),
        P("fsdp"),
        P("fsdp", None),
        P("fsdp", None),
        P("fsdp"),
        P("fsdp", None),
        P("fsdp", None),
        P("fsdp", None),
        P("fsdp", None, "rep"),
        P("fsdp", None, "rep"),
        P("fsdp", "rep", None),
    )
    out_specs = (
        P("rep", "fsdp", None),
        P("rep", "fsdp", None),
        P("fsdp"),
        P("fsdp", None),
        P("fsdp", None),
        P("fsdp"),
        P("fsdp", None),
        P("fsdp", None),
        P("fsdp"),
        P("fsdp", None),
        P("fsdp", None),
        P("fsdp", None),
        P("fsdp", None, "rep"),
        P("fsdp", None, "rep"),
        P("fsdp", "rep", None),
    )
    return jax.shard_map(body, mesh=mesh, in_specs=in_specs, out_specs=out_specs, check_vma=False)
```

profile of v0, /device:TPU:0, one launch (start us, length us, event | category | flops | bytes accessed | tf_op | source)
XLA Modules:
  0.0 1074.3 jit_solution(3285041317513848760)
XLA Ops:
  9.2 5.1 collective-permute-start.15
  20.7 6.7 all-to-all-start
  47.3 17.6 %collective-permute-done.18 = bf16[4,128,640]{1,2,0:T(8,128)(2,1)S(1)} collective-permute-done((bf16[4,128,640]{1,2,0:T(8,128)(2,1)S(1)}, bf16[4,128,640]{1,2,0:T(8,128)(2,1)S(1)}, u32[]{:S(2)}, u32[]{:S(2)}) %collective-permute-start.18) | collective-permute-done | bytes 655392 | tf_op jit(solution)/shard_map/small/ppermute | solution.py:75
  67.0 28.6 %collective-permute-done.1 = bf16[128,2048]{1,0:T(8,128)(2,1)S(1)} collective-permute-done((bf16[128,2048]{1,0:T(8,128)(2,1)S(1)}, bf16[128,2048]{1,0:T(8,128)(2,1)S(1)}, u32[]{:S(2)}, u32[]{:S(2)}) %collective-permute-start.1) | collective-permute-done | bytes 524320 | tf_op jit(solution)/shard_map/hidden/ppermute | solution.py:75
  99.6 7.0 collective-permute-done.21
  127.2 9.2 collective-permute-done.7
  150.5 5.0 fusion.123
  159.3 6.3 pad_maximum_fusion
  179.1 5.8 collective-permute-done.22.refs_10_.refs_9_
  185.9 31.8 %shard_map.307 = (bf16[16,128,128]{2,1,0:T(8,128)(2,1)}, bf16[2,1024,128]{2,1,0:T(8,128)(2,1)}, bf16[2,1024,128]{2,1,0:T(8,128)(2,1)}, bf16[2,1024,128]{2,1,0:T(...) custom-call(s32[16]{0:T(128)} %copy-done.93, ...), custom_call_target="tpu_custom_call" | custom-call | flops 9663676416 | bytes 21184512 | tf_op jit(solution)/shard_map/pallas_call | solution.py:250
  217.7 6.5 all-to-all-start.1
  233.5 11.2 %collective-permute-done.8 = bf16[128,2048]{1,0:T(8,128)(2,1)S(1)} collective-permute-done((bf16[128,2048]{1,0:T(8,128)(2,1)S(1)}, bf16[128,2048]{1,0:T(8,128)(2,1)S(1)}, u32[]{:S(2)}, u32[]{:S(2)}) %collective-permute-start.8) | collective-permute-done | bytes 524320 | tf_op jit(solution)/shard_map/cotangent/ppermute | solution.py:75
  275.2 4.4 all-to-all-start.2
  279.7 28.4 %collective-permute-done.33 = bf16[128,2048]{1,0:T(8,128)(2,1)} collective-permute-done((bf16[128,2048]{1,0:T(8,128)(2,1)S(1)}, bf16[128,2048]{1,0:T(8,128)(2,1)}, u32[]{:S(2)}, u32[]{:S(2)}) %collective-permute-start.33) | collective-permute-done | bytes 524320 | tf_op jit(solution)/shard_map/cotangent/ppermute | solution.py:75
  321.3 19.1 %collective-permute-done.36.refs_3_ = bf16[2,128,2048]{2,1,0:T(8,128)(2,1)S(1)} collective-permute-done((bf16[2,128,2048]{2,1,0:T(8,128)(2,1)}, bf16[2,128,2048]{2,1,0:T(8,128)(2,1)S(1)}, u32[]{:S(2)}, u32[]{:S(2)}) %collective-permute-start.36) | collective-permute-done | bytes 1048608 | tf_op jit(solution)/shard_map/cotangent/ppermute | solution.py:75
  343.3 5.9 collective-permute-done.38.refs_6_
  358.5 7.5 collective-permute-done.40.refs_8_
  367.2 19.9 %shard_map.308 = (bf16[576,2048]{1,0:T(8,128)(2,1)}, f32[576,1408]{1,0:T(8,128)}, f32[1024,176]{1,0:T(8,128)}, bf16[1024,2048]{1,0:T(8,128)(2,1)}) custom-call(bf16[2,128,2048]{2,1,0:T(8,128)(2,1)} %copy-done.15, bf16[2,128,2048]{2,1,0:T(8,128)(2,1)} %pad_maximum_fusion.13.refs_1_, bf16[2,128,2048]{2,1,0:T(8,128)(2,1)} %collective-permute-done.34.refs_2_, ...), custom_call_target="tpu_custom_call" | custom-call | flops 3925868544 | bytes 19759104 | tf_op jit(solution)/shard_map/pallas_call | solution.py:250
  387.1 7.5 collective-permute-done.29
  403.4 19.9 %shard_map.309 = (bf16[576,2048]{1,0:T(8,128)(2,1)}, f32[576,1408]{1,0:T(8,128)}, f32[1024,176]{1,0:T(8,128)}, bf16[1024,2048]{1,0:T(8,128)(2,1)}) custom-call(bf16[2,128,2048]{2,1,0:T(8,128)(2,1)} %copy-done.15, bf16[2,128,2048]{2,1,0:T(8,128)(2,1)} %pad_maximum_fusion.13.refs_1_, bf16[2,128,2048]{2,1,0:T(8,128)(2,1)} %collective-permute-done.34.refs_2_, ...), custom_call_target="tpu_custom_call" | custom-call | flops 3925868544 | bytes 19759104 | tf_op jit(solution)/shard_map/pallas_call | solution.py:250
  426.3 5.2 collective-permute-done.44.refs_6_
  435.7 9.4 collective-permute-done.46.refs_8_
  449.8 39.7 %shard_map.310 = (bf16[1024,2048]{1,0:T(8,128)(2,1)}, bf16[576,2048]{1,0:T(8,128)(2,1)}, bf16[576,1408]{1,0:T(8,128)(2,1)}, bf16[576,2816]{1,0:T(8,128)(2,1)}, b...) custom-call(bf16[2,128,2048]{2,1,0:T(8,128)(2,1)} %pad_maximum_fusio, ...), custom_call_target="tpu_custom_call" | custom-call | flops 17582522368 | bytes 32227328 | tf_op jit(solution)/shard_map/pallas_call | solution.py:250
  489.5 39.3 %shard_map.311 = (bf16[1024,2048]{1,0:T(8,128)(2,1)}, bf16[576,2048]{1,0:T(8,128)(2,1)}, bf16[576,1408]{1,0:T(8,128)(2,1)}, bf16[576,2816]{1,0:T(8,128)(2,1)}, b...) custom-call(bf16[2,128,2048]{2,1,0:T(8,128)(2,1)} %pad_maximum_fusio, ...), custom_call_target="tpu_custom_call", output_to_operand_aliasing={{7}: (16, {}), {8}: (17, {}), {9}: (18, {}), {10}: (19, {})... | custom-call | flops 17582522368 | bytes 32227328 | tf_op jit(solution)/shard_map/pallas_call | solution.py:250
  545.0 12.7 %shard_map.312 = (bf16[2,128,2048]{2,1,0:T(8,128)(2,1)}, bf16[2,128,2048]{2,1,0:T(8,128)(2,1)}, bf16[2,128,2048]{2,1,0:T(8,128)(2,1)}, bf16[2,128,2048]{2,1,0:T(...) custom-call(bf16[576,1408]{1,0:T(8,128)(2,1)} %get-tuple-element.251, ...), custom_call_target="tpu_custom_call" | custom-call | flops 5469372416 | bytes 11583488 | tf_op jit(solution)/shard_map/pallas_call | solution.py:250
  557.6 15.4 %shard_map.313.refs_17_ = bf16[2,704,2048]{2,1,0:T(8,128)(2,1)} custom-call(bf16[2,128,2048]{2,1,0:T(8,128)(2,1)} %fusion.50.refs_0_, bf16[2,128,2048]{2,1,0:T(8,128)(2,1)} %get-tuple-element.255.refs_1_.refs_6_, bf16[576,1408]{1,0:T(8,128)(2,1)} %get-tuple-element.251.refs_0_.refs_2_, bf16[576,1408]{1,0:T(8,128)(2,1)} %get-tuple-element.249.refs_3_.refs_0_, ...), custom_call_target="tpu_custom_call" | custom-call | flops 6643777536 | bytes 28835840 | tf_op jit(solution)/shard_map/pallas_call | solution.py:660
  577.0 11.7 %collective-permute-done.50 = bf16[1,128,2048]{2,1,0:T(8,128)(2,1)S(1)} collective-permute-done((bf16[1,128,2048]{2,1,0:T(8,128)(2,1)}, bf16[1,128,2048]{2,1,0:T(8,128)(2,1)S(1)}, u32[]{:S(2)}, u32[]{:S(2)}) %collective-permute-start.50) | collective-permute-done | bytes 524320 | tf_op jit(solution)/shard_map/grad_mixed/ppermute | solution.py:79
  596.2 14.9 %collective-permute-done.49 = bf16[2,128,2048]{2,1,0:T(8,128)(2,1)S(1)} collective-permute-done((bf16[2,128,2048]{2,1,0:T(8,128)(2,1)}, bf16[2,128,2048]{2,1,0:T(8,128)(2,1)S(1)}, u32[]{:S(2)}, u32[]{:S(2)}) %collective-permute-start.49) | collective-permute-done | bytes 1048608 | tf_op jit(solution)/shard_map/grad_mixed/ppermute | solution.py:79
  611.2 5.8 collective-permute-done.51
  618.6 10.9 %collective-permute-done.54 = bf16[2,128,2048]{2,1,0:T(8,128)(2,1)S(1)} collective-permute-done((bf16[2,128,2048]{2,1,0:T(8,128)(2,1)}, bf16[2,128,2048]{2,1,0:T(8,128)(2,1)S(1)}, u32[]{:S(2)}, u32[]{:S(2)}) %collective-permute-start.54) | collective-permute-done | bytes 1048608 | tf_op jit(solution)/shard_map/grad_mixed/ppermute | solution.py:79
  630.7 12.2 %shard_map.314 = (bf16[2,128,2048]{2,1,0:T(8,128)(2,1)}, bf16[2,128,2048]{2,1,0:T(8,128)(2,1)}, bf16[2,128,2048]{2,1,0:T(8,128)(2,1)}, bf16[2,128,2048]{2,1,0:T(...) custom-call(bf16[576,1408]{1,0:T(8,128)(2,1)} %get-tuple-element.249, ...), custom_call_target="tpu_custom_call", output_to_operand_aliasing={{0}: (6, {}), {1}: (7, {}), {2}: (8, {}), {3}: (9, {}), {4}... | custom-call | flops 5469372416 | bytes 11583488 | tf_op jit(solution)/shard_map/pallas_call | solution.py:250
  643.0 6.9 collective-permute-done.57
  652.6 24.2 %shard_map.315 = (bf16[2,704,2048]{2,1,0:T(8,128)(2,1)}, bf16[2,704,2048]{2,1,0:T(8,128)(2,1)}) custom-call(f32[128,2048]{1,0:T(8,128)} %get-tuple-element.455.refs_0_, bf16[2,128,2048]{2,1,0:T(8,128)(2,1)} %get-tuple-element.275.refs_1_, bf16[576,2816]{1,0:T(8,128)(2,1)} %get-tuple-element.284.refs_2_, bf16[576,2816]{1,0:T(8,128)(2,1)} %get-tuple-element.285.refs_3_, ...), custom_call_target="tpu_custom_call" | custom-call | flops 13287555072 | bytes 28835840 | tf_op jit(solution)/shard_map/pallas_call | solution.py:660
  676.9 4.4 fusion.40
  683.6 37.9 %all_to_all.35 = bf16[16,128,352]{1,2,0:T(8,128)(2,1)} all-to-all(bf16[16,128,352]{1,2,0:T(8,128)(2,1)S(1)} %bitcast.381), channel_id=1, replica_groups=mesh['rep'=2,'fsdp'=16] {'fsdp'}, dimensions={0} | all-to-all | bytes 2883584 | tf_op jit(solution)/shard_map/all_to_all | solution.py:743
  747.7 4.5 add_convert_fusion
  755.3 7.8 all-to-all-done.4.refs_11_
  765.6 28.6 %shard_map.316 = (bf16[16,128,256]{2,1,0:T(8,128)(2,1)}, bf16[4,128,640]{2,1,0:T(8,128)(2,1)}, bf16[4,128,640]{2,1,0:T(8,128)(2,1)}, bf16[4,128,640]{2,1,0:T(8,1...) custom-call(s32[16]{0:T(128)} %copy-done.93, ...), custom_call_target="tpu_custom_call" | custom-call | flops 8589934592 | bytes 30212096 | tf_op jit(solution)/shard_map/pallas_call | solution.py:250
  808.4 4.7 all-to-all-start.5
  826.0 23.1 %collective-permute-done.63 = bf16[1,128,2048]{2,1,0:T(8,128)(2,1)} collective-permute-done((bf16[1,128,2048]{2,1,0:T(8,128)(2,1)}, bf16[1,128,2048]{2,1,0:T(8,128)(2,1)}, u32[]{:S(2)}, u32[]{:S(2)}) %collective-permute-start.63) | collective-permute-done | bytes 524320 | tf_op jit(solution)/shard_map/routed/ppermute | solution.py:79
  859.0 6.4 collective-permute-done.68
  868.1 19.8 %collective-permute-done.64 = bf16[2,128,2048]{2,1,0:T(8,128)(2,1)S(1)} collective-permute-done((bf16[2,128,2048]{2,1,0:T(8,128)(2,1)S(1)}, bf16[2,128,2048]{2,1,0:T(8,128)(2,1)S(1)}, u32[]{:S(2)}, u32[]{:S(2)}) %collective-permute-start.64) | collective-permute-done | bytes 1048608 | tf_op jit(solution)/shard_map/routed/ppermute | solution.py:79
  896.3 13.3 %collective-permute-done.60 = bf16[2,128,2048]{2,1,0:T(8,128)(2,1)} collective-permute-done((bf16[2,128,2048]{2,1,0:T(8,128)(2,1)}, bf16[2,128,2048]{2,1,0:T(8,128)(2,1)}, u32[]{:S(2)}, u32[]{:S(2)}) %collective-permute-start.60) | collective-permute-done | bytes 1048608 | tf_op jit(solution)/shard_map/routed/ppermute | solution.py:79
  931.2 5.3 all-to-all-start.6
  938.3 5.0 fusion
  943.4 6.1 fusion.30
  987.5 22.0 %collective-permute-start.90 = (bf16[128,1024]{1,0:T(8,128)(2,1)S(1)}, bf16[128,1024]{1,0:T(8,128)(2,1)S(1)}, u32[]{:S(2)}, u32[]{:S(2)}) collective-permute-start(bf16[128,1024]{1,0:T(8,128)(2,1)S(1)} %get-tuple-element.490), channel_id=1, source_target_pairs={{0,4},{1,5},{2,6},{3,7},{4,8},{5,9},{6,10},{7,11},{8,12},{9,13},{1... | collective-permute-start | bytes 786440 | tf_op jit(solution)/shard_map/grad_output_w/ppermute | solution.py:79
  1009.5 12.8 %collective-permute-done.75 = bf16[128,2048]{1,0:T(8,128)(2,1)} collective-permute-done((bf16[128,2048]{1,0:T(8,128)(2,1)}, bf16[128,2048]{1,0:T(8,128)(2,1)}, u32[]{:S(2)}, u32[]{:S(2)}) %collective-permute-start.75) | collective-permute-done | bytes 524320 | tf_op jit(solution)/shard_map/routed/ppermute | solution.py:79
  (693 shorter events, 394.2 us)
Async XLA Ops:
  7.2 143.3 %all-gather.20.cloned.1.call-start = ((), (), s32[]{:S(2)}) async-start(), calls=%async_computation.15 | async-start | bytes 8650752 | tf_op jit(solution)/shard_map/all_gather | solution.py:810
  7.9 147.6 %all-gather.22.cloned.1.call-start = ((), (), s32[]{:S(2)}) async-start(), calls=%async_computation.16 | async-start | bytes 8650752 | tf_op jit(solution)/shard_map/all_gather | solution.py:810
  18.2 48.2 %collective-permute-start = (bf16[128,2048]{1,0:T(8,128)(2,1)S(1)}, bf16[128,2048]{1,0:T(8,128)(2,1)}, u32[]{:S(2)}, u32[]{:S(2)}) collective-permute-start(bf16[128,2048]{1,0:T(8,128)(2,1)S(1)} %bitcast.371), channel_id=1, source_target_pairs={{12,0},{13,1},{14,2},{15,3},{0,4},{1,5},{2,6},{3,7},{4,8},{5,9},{6... | collective-permute-start | bytes 1572872 | tf_op jit(solution)/shard_map/hidden/ppermute | solution.py:75
  20.7 118.0 %all-to-all-start = ((bf16[16,128,256]{1,2,0:T(8,128)(2,1)}), bf16[16,128,256]{1,2,0:T(8,128)(2,1)}, u32[]{:S(2)}, u32[]{:S(2)}) async-start(bf16[16,128,256]{1,2,0:T(8,128)(2,1)} %pad_maximum_fusion.9), calls=%async_computation | async-start | bytes 2097152 | tf_op jit(solution)/shard_map/all_to_all | solution.py:743
  27.4 138.3 %all-gather.16.cloned.1.call-start = ((), (), s32[]{:S(2)}) async-start(), calls=%async_computation.10 | async-start | bytes 8650752 | tf_op jit(solution)/shard_map/all_gather | solution.py:810
  38.7 57.0 %collective-permute-start.1 = (bf16[128,2048]{1,0:T(8,128)(2,1)S(1)}, bf16[128,2048]{1,0:T(8,128)(2,1)S(1)}, u32[]{:S(2)}, u32[]{:S(2)}) collective-permute-start(bf16[128,2048]{1,0:T(8,128)(2,1)S(1)} %bitcast.372), channel_id=1, source_target_pairs={{8,0},{9,1},{10,2},{11,3},{12,4},{13,5},{14,6},{15,7},{0,8},{1,9},... | collective-permute-start | bytes 1572872 | tf_op jit(solution)/shard_map/hidden/ppermute | solution.py:75
  43.1 54.7 %collective-permute-start.19 = (bf16[4,128,640]{1,2,0:T(8,128)(2,1)S(1)}, bf16[4,128,640]{1,2,0:T(8,128)(2,1)S(1)}, u32[]{:S(2)}, u32[]{:S(2)}) collective-permute-start(bf16[4,128,640]{1,2,0:T(8,128)(2,1)S(1)} %pad_maximum_fusion.15), channel_id=1, source_target_pairs={{2,0},{3,1},{0,2},{1,3},{6,4},{7,5},{4,6},{5,7},{10,8},{11,9},{8,1... | collective-permute-start | bytes 1966088 | tf_op jit(solution)/shard_map/small/ppermute | solution.py:75
  46.8 68.4 %collective-permute-start.3 = (bf16[2,128,2048]{2,1,0:T(8,128)(2,1)}, bf16[2,128,2048]{2,1,0:T(8,128)(2,1)}, u32[]{:S(2)}, u32[]{:S(2)}) collective-permute-start(bf16[2,128,2048]{2,1,0:T(8,128)(2,1)} %pad_maximum_fusion.6.refs_2_.refs_1_), channel_id=1, source_target_pairs={{1,0},{0,1},{3,2},{2,3},{5,4},{4,5},{7,6},{6,7},{9,8},{8,9},{11,10... | collective-permute-start | bytes 3145736 | tf_op jit(solution)/shard_map/hidden/ppermute | solution.py:75
  64.9 50.3 %collective-permute-start.4 = (bf16[2,128,2048]{2,1,0:T(8,128)(2,1)}, bf16[2,128,2048]{2,1,0:T(8,128)(2,1)}, u32[]{:S(2)}, u32[]{:S(2)}) collective-permute-start(bf16[2,128,2048]{2,1,0:T(8,128)(2,1)} %pad_maximum_fusion.6.refs_2_.refs_1_), channel_id=1, source_target_pairs={{2,0},{3,1},{0,2},{1,3},{6,4},{7,5},{4,6},{5,7},{10,8},{11,9},{8,1... | collective-permute-start | bytes 3145736 | tf_op jit(solution)/shard_map/hidden/ppermute | solution.py:75
  136.5 35.5 %collective-permute-start.13 = (bf16[1,128,2048]{2,1,0:T(8,128)(2,1)}, bf16[1,128,2048]{2,1,0:T(8,128)(2,1)}, u32[]{:S(2)}, u32[]{:S(2)}) collective-permute-start(bf16[1,128,2048]{2,1,0:T(8,128)(2,1)} %slice.562), channel_id=1, source_target_pairs={{2,0},{3,1},{0,2},{1,3},{6,4},{7,5},{4,6},{5,7},{10,8},{11,9},{8,1... | collective-permute-start | bytes 1572872 | tf_op jit(solution)/shard_map/hidden/ppermute | solution.py:75
  137.0 35.0 %collective-permute-start.14 = (bf16[1,128,2048]{2,1,0:T(8,128)(2,1)}, bf16[1,128,2048]{2,1,0:T(8,128)(2,1)}, u32[]{:S(2)}, u32[]{:S(2)}) collective-permute-start(bf16[1,128,2048]{2,1,0:T(8,128)(2,1)} %slice.563), channel_id=1, source_target_pairs={{1,0},{0,1},{3,2},{2,3},{5,4},{4,5},{7,6},{6,7},{9,8},{8,9},{11,10... | collective-permute-start | bytes 1572872 | tf_op jit(solution)/shard_map/hidden/ppermute | solution.py:75
  255.8 52.3 %collective-permute-start.33 = (bf16[128,2048]{1,0:T(8,128)(2,1)S(1)}, bf16[128,2048]{1,0:T(8,128)(2,1)}, u32[]{:S(2)}, u32[]{:S(2)}) collective-permute-start(bf16[128,2048]{1,0:T(8,128)(2,1)S(1)} %bitcast.377), channel_id=1, source_target_pairs={{8,0},{9,1},{10,2},{11,3},{12,4},{13,5},{14,6},{15,7},{0,8},{1,9},... | collective-permute-start | bytes 1572872 | tf_op jit(solution)/shard_map/cotangent/ppermute | solution.py:75
  257.9 52.5 %collective-permute-start.34 = (bf16[2,128,2048]{2,1,0:T(8,128)(2,1)S(1)}, bf16[2,128,2048]{2,1,0:T(8,128)(2,1)}, u32[]{:S(2)}, u32[]{:S(2)}) collective-permute-start(bf16[2,128,2048]{2,1,0:T(8,128)(2,1)S(1)} %pad_maximum_fusion.8.refs_0_), channel_id=1, source_target_pairs={{1,0},{0,1},{3,2},{2,3},{5,4},{4,5},{7,6},{6,7},{9,8},{8,9},{11,10... | collective-permute-start | bytes 3145736 | tf_op jit(solution)/shard_map/cotangent/ppermute | solution.py:75
  258.4 51.9 %collective-permute-start.35 = (bf16[2,128,2048]{2,1,0:T(8,128)(2,1)S(1)}, bf16[2,128,2048]{2,1,0:T(8,128)(2,1)}, u32[]{:S(2)}, u32[]{:S(2)}) collective-permute-start(bf16[2,128,2048]{2,1,0:T(8,128)(2,1)S(1)} %pad_maximum_fusion.8.refs_0_), channel_id=1, source_target_pairs={{2,0},{3,1},{0,2},{1,3},{6,4},{7,5},{4,6},{5,7},{10,8},{11,9},{8,1... | collective-permute-start | bytes 3145736 | tf_op jit(solution)/shard_map/cotangent/ppermute | solution.py:75
  275.2 119.5 %all-to-all-start.2 = ((bf16[16,128,352]{1,2,0:T(8,128)(2,1)}), bf16[16,128,352]{1,2,0:T(8,128)(2,1)}, u32[]{:S(2)}, u32[]{:S(2)}) async-start(bf16[16,128,352]{1,2,0:T(8,128)(2,1)} %pad_maximum_fusion.3), calls=%async_computation.2 | async-start | bytes 2883584 | tf_op jit(solution)/shard_map/all_to_all | solution.py:743
  279.6 441.9 %all-gather.18.cloned.1.call-start = ((), (), s32[]{:S(2)}) async-start(), calls=%async_computation.11 | async-start | bytes 6684672 | tf_op jit(solution)/shard_map/all_gather | solution.py:903
  314.1 35.0 %collective-permute-start.38 = (bf16[1,128,2048]{2,1,0:T(8,128)(2,1)}, bf16[1,128,2048]{2,1,0:T(8,128)(2,1)}, u32[]{:S(2)}, u32[]{:S(2)}) collective-permute-start(bf16[1,128,2048]{2,1,0:T(8,128)(2,1)} %slice.585), channel_id=1, source_target_pairs={{2,0},{3,1},{0,2},{1,3},{6,4},{7,5},{4,6},{5,7},{10,8},{11,9},{8,1... | collective-permute-start | bytes 1572872 | tf_op jit(solution)/shard_map/cotangent/ppermute | solution.py:75
  316.8 34.0 %collective-permute-start.39 = (bf16[1,128,2048]{2,1,0:T(8,128)(2,1)}, bf16[1,128,2048]{2,1,0:T(8,128)(2,1)}, u32[]{:S(2)}, u32[]{:S(2)}) collective-permute-start(bf16[1,128,2048]{2,1,0:T(8,128)(2,1)} %slice.586), channel_id=1, source_target_pairs={{1,0},{0,1},{3,2},{2,3},{5,4},{4,5},{7,6},{6,7},{9,8},{8,9},{11,10... | collective-permute-start | bytes 1572872 | tf_op jit(solution)/shard_map/cotangent/ppermute | solution.py:75
  318.3 34.0 %collective-permute-start.27 = (bf16[128,2048]{1,0:T(8,128)(2,1)}, bf16[128,2048]{1,0:T(8,128)(2,1)}, u32[]{:S(2)}, u32[]{:S(2)}) collective-permute-start(bf16[128,2048]{1,0:T(8,128)(2,1)} %multiply_convert_fusion.1.refs_14_), channel_id=1, source_target_pairs={{4,0},{5,1},{6,2},{7,3},{8,4},{9,5},{10,6},{11,7},{12,8},{13,9},{1... | collective-permute-start | bytes 1572872 | tf_op jit(solution)/shard_map/mixed/ppermute | solution.py:75
  354.6 40.1 %collective-permute-start.30 = (bf16[2,128,2048]{2,1,0:T(8,128)(2,1)}, bf16[2,128,2048]{2,1,0:T(8,128)(2,1)}, u32[]{:S(2)}, u32[]{:S(2)}) collective-permute-start(bf16[2,128,2048]{2,1,0:T(8,128)(2,1)} %pad_maximum_fusion.11.refs_0_), channel_id=1, source_target_pairs={{1,0},{0,1},{3,2},{2,3},{5,4},{4,5},{7,6},{6,7},{9,8},{8,9},{11,10... | collective-permute-start | bytes 3145736 | tf_op jit(solution)/shard_map/mixed/ppermute | solution.py:75
  356.3 38.4 %collective-permute-start.31 = (bf16[2,128,2048]{2,1,0:T(8,128)(2,1)}, bf16[2,128,2048]{2,1,0:T(8,128)(2,1)}, u32[]{:S(2)}, u32[]{:S(2)}) collective-permute-start(bf16[2,128,2048]{2,1,0:T(8,128)(2,1)} %pad_maximum_fusion.11.refs_0_), channel_id=1, source_target_pairs={{2,0},{3,1},{0,2},{1,3},{6,4},{7,5},{4,6},{5,7},{10,8},{11,9},{8,1... | collective-permute-start | bytes 3145736 | tf_op jit(solution)/shard_map/mixed/ppermute | solution.py:75
  445.9 287.5 %all-gather.30.cloned.1.call-start = ((), (), s32[]{:S(2)}) async-start(), calls=%async_computation.20 | async-start | bytes 2162688 | tf_op jit(solution)/shard_map/all_gather | solution.py:693
  537.1 226.0 %reduce-scatter.8.cloned.1.call-start = ((), (), s32[]{:S(2)}) async-start(), calls=%async_computation.14 | async-start | bytes 8650752 | tf_op jit(solution)/shard_map/reduce_scatter | solution.py:954
  573.1 190.1 %reduce-scatter.6.cloned.1.call-start = ((), (), s32[]{:S(2)}) async-start(), calls=%async_computation.13 | async-start | bytes 8650752 | tf_op jit(solution)/shard_map/reduce_scatter | solution.py:954
  576.4 34.7 %collective-permute-start.49 = (bf16[2,128,2048]{2,1,0:T(8,128)(2,1)}, bf16[2,128,2048]{2,1,0:T(8,128)(2,1)S(1)}, u32[]{:S(2)}, u32[]{:S(2)}) collective-permute-start(bf16[2,128,2048]{2,1,0:T(8,128)(2,1)} %fusion.48.refs_6_), channel_id=1, source_target_pairs={{0,1},{1,0},{2,3},{3,2},{4,5},{5,4},{6,7},{7,6},{8,9},{9,8},{10,11... | collective-permute-start | bytes 3145736 | tf_op jit(solution)/shard_map/grad_mixed/ppermute | solution.py:79
  594.0 35.5 %collective-permute-start.54 = (bf16[2,128,2048]{2,1,0:T(8,128)(2,1)}, bf16[2,128,2048]{2,1,0:T(8,128)(2,1)S(1)}, u32[]{:S(2)}, u32[]{:S(2)}) collective-permute-start(bf16[2,128,2048]{2,1,0:T(8,128)(2,1)} %fusion.51), channel_id=1, source_target_pairs={{0,1},{1,0},{2,3},{3,2},{4,5},{5,4},{6,7},{7,6},{8,9},{9,8},{10,11... | collective-permute-start | bytes 3145736 | tf_op jit(solution)/shard_map/grad_mixed/ppermute | solution.py:79
  595.5 34.9 %collective-permute-start.55 = (bf16[2,128,2048]{2,1,0:T(8,128)(2,1)S(1)}, bf16[2,128,2048]{2,1,0:T(8,128)(2,1)S(1)}, u32[]{:S(2)}, u32[]{:S(2)}) collective-permute-start(bf16[2,128,2048]{2,1,0:T(8,128)(2,1)S(1)} %copy-done.73), channel_id=1, source_target_pairs={{0,2},{1,3},{2,0},{3,1},{4,6},{5,7},{6,4},{7,5},{8,10},{9,11},{10,... | collective-permute-start | bytes 3145736 | tf_op jit(solution)/shard_map/grad_mixed/ppermute | solution.py:79
  676.8 86.3 %reduce-scatter.4.cloned.1.call-start = ((), (), s32[]{:S(2)}) async-start(), calls=%async_computation.12 | async-start | bytes 8650752 | tf_op jit(solution)/shard_map/reduce_scatter | solution.py:954
  721.5 44.1 %all-gather.24.cloned.1.call-start = ((), (), s32[]{:S(2)}) async-start(), calls=%async_computation.17 | async-start | bytes 18874368 | tf_op jit(solution)/shard_map/all_gather | solution.py:952
  808.4 82.3 %all-to-all-start.5 = ((bf16[16,128,256]{2,1,0:T(8,128)(2,1)}), bf16[16,128,256]{2,1,0:T(8,128)(2,1)S(1)}, u32[]{:S(2)}, u32[]{:S(2)}) async-start(bf16[16,128,256]{2,1,0:T(8,128)(2,1)} %get-tuple-element.324), calls=%async_computation.8 | async-start | bytes 2097152 | tf_op jit(solution)/shard_map/all_to_all | solution.py:743
  813.1 217.6 %all-gather.28.cloned.1.call-start = ((), (), s32[]{:S(2)}) async-start(), calls=%async_computation.19 | async-start | bytes 4325376 | tf_op jit(solution)/shard_map/all_gather | solution.py:693
  813.4 40.1 %collective-permute-start.59 = (bf16[1,128,2048]{2,1,0:T(8,128)(2,1)}, bf16[1,128,2048]{2,1,0:T(8,128)(2,1)}, u32[]{:S(2)}, u32[]{:S(2)}) collective-permute-start(bf16[1,128,2048]{2,1,0:T(8,128)(2,1)} %get-tuple-element.308), channel_id=1, source_target_pairs={{0,2},{1,3},{2,0},{3,1},{4,6},{5,7},{6,4},{7,5},{8,10},{9,11},{10,... | collective-permute-start | bytes 1572872 | tf_op jit(solution)/shard_map/routed/ppermute | solution.py:79
  815.3 41.0 %collective-permute-start.61 = (bf16[1,128,2048]{2,1,0:T(8,128)(2,1)}, bf16[1,128,2048]{2,1,0:T(8,128)(2,1)S(1)}, u32[]{:S(2)}, u32[]{:S(2)}) collective-permute-start(bf16[1,128,2048]{2,1,0:T(8,128)(2,1)} %get-tuple-element.310), channel_id=1, source_target_pairs={{0,1},{1,0},{2,3},{3,2},{4,5},{5,4},{6,7},{7,6},{8,9},{9,8},{10,11... | collective-permute-start | bytes 1572872 | tf_op jit(solution)/shard_map/routed/ppermute | solution.py:79
  822.9 42.6 %collective-permute-start.68 = (bf16[4,128,640]{2,1,0:T(8,128)(2,1)}, bf16[4,128,640]{2,1,0:T(8,128)(2,1)S(1)}, u32[]{:S(2)}, u32[]{:S(2)}) collective-permute-start(bf16[4,128,640]{2,1,0:T(8,128)(2,1)} %fusion.69), channel_id=1, source_target_pairs={{0,1},{1,0},{2,3},{3,2},{4,5},{5,4},{6,7},{7,6},{8,9},{9,8},{10,11... | collective-permute-start | bytes 1966088 | tf_op jit(solution)/shard_map/grad_latent/ppermute | solution.py:79
  851.4 36.5 %collective-permute-start.64 = (bf16[2,128,2048]{2,1,0:T(8,128)(2,1)S(1)}, bf16[2,128,2048]{2,1,0:T(8,128)(2,1)S(1)}, u32[]{:S(2)}, u32[]{:S(2)}) collective-permute-start(bf16[2,128,2048]{2,1,0:T(8,128)(2,1)S(1)} %fusion.56), channel_id=1, source_target_pairs={{0,1},{1,0},{2,3},{3,2},{4,5},{5,4},{6,7},{7,6},{8,9},{9,8},{10,11... | collective-permute-start | bytes 3145736 | tf_op jit(solution)/shard_map/routed/ppermute | solution.py:79
  853.5 35.7 %collective-permute-start.66 = (bf16[2,128,2048]{2,1,0:T(8,128)(2,1)S(1)}, bf16[2,128,2048]{2,1,0:T(8,128)(2,1)S(1)}, u32[]{:S(2)}, u32[]{:S(2)}) collective-permute-start(bf16[2,128,2048]{2,1,0:T(8,128)(2,1)S(1)} %fusion.57), channel_id=1, source_target_pairs={{0,2},{1,3},{2,0},{3,1},{4,6},{5,7},{6,4},{7,5},{8,10},{9,11},{10,... | collective-permute-start | bytes 3145736 | tf_op jit(solution)/shard_map/routed/ppermute | solution.py:79
  856.4 53.2 %collective-permute-start.60 = (bf16[2,128,2048]{2,1,0:T(8,128)(2,1)}, bf16[2,128,2048]{2,1,0:T(8,128)(2,1)}, u32[]{:S(2)}, u32[]{:S(2)}) collective-permute-start(bf16[2,128,2048]{2,1,0:T(8,128)(2,1)} %fusion.54), channel_id=1, source_target_pairs={{0,1},{1,0},{2,3},{3,2},{4,5},{5,4},{6,7},{7,6},{8,9},{9,8},{10,11... | collective-permute-start | bytes 3145736 | tf_op jit(solution)/shard_map/routed/ppermute | solution.py:79
  865.4 44.4 %collective-permute-start.62 = (bf16[2,128,2048]{2,1,0:T(8,128)(2,1)}, bf16[2,128,2048]{2,1,0:T(8,128)(2,1)}, u32[]{:S(2)}, u32[]{:S(2)}) collective-permute-start(bf16[2,128,2048]{2,1,0:T(8,128)(2,1)} %fusion.55), channel_id=1, source_target_pairs={{0,2},{1,3},{2,0},{3,1},{4,6},{5,7},{6,4},{7,5},{8,10},{9,11},{10,... | collective-permute-start | bytes 3145736 | tf_op jit(solution)/shard_map/routed/ppermute | solution.py:79
  919.8 45.0 %collective-permute-start.79 = (bf16[128,576]{1,0:T(8,128)(2,1)}, bf16[128,576]{1,0:T(8,128)(2,1)}, u32[]{:S(2)}, u32[]{:S(2)}) collective-permute-start(bf16[128,576]{1,0:T(8,128)(2,1)} %pad_maximum_fusion.19), channel_id=1, source_target_pairs={{4,0},{5,1},{6,2},{7,3},{8,4},{9,5},{10,6},{11,7},{12,8},{13,9},{1... | collective-permute-start | bytes 442376 | tf_op jit(solution)/shard_map/grad_kv/ppermute | solution.py:75
  923.0 46.1 %collective-permute-start.80 = (bf16[128,576]{1,0:T(8,128)(2,1)}, bf16[128,576]{1,0:T(8,128)(2,1)}, u32[]{:S(2)}, u32[]{:S(2)}) collective-permute-start(bf16[128,576]{1,0:T(8,128)(2,1)} %pad_maximum_fusion.19), channel_id=1, source_target_pairs={{12,0},{13,1},{14,2},{15,3},{0,4},{1,5},{2,6},{3,7},{4,8},{5,9},{6... | collective-permute-start | bytes 442376 | tf_op jit(solution)/shard_map/grad_kv/ppermute | solution.py:75
  923.0 47.9 %collective-permute-start.81 = (bf16[128,576]{1,0:T(8,128)(2,1)}, bf16[128,576]{1,0:T(8,128)(2,1)}, u32[]{:S(2)}, u32[]{:S(2)}) collective-permute-start(bf16[128,576]{1,0:T(8,128)(2,1)} %pad_maximum_fusion.19), channel_id=1, source_target_pairs={{8,0},{9,1},{10,2},{11,3},{12,4},{13,5},{14,6},{15,7},{0,8},{1,9},... | collective-permute-start | bytes 442376 | tf_op jit(solution)/shard_map/grad_kv/ppermute | solution.py:75
  931.2 109.7 %all-to-all-start.6 = ((bf16[16,144,256]{2,1,0:T(8,128)(2,1)}), bf16[16,144,256]{2,1,0:T(8,128)(2,1)}, u32[]{:S(2)}, u32[]{:S(2)}) async-start(bf16[16,144,256]{2,1,0:T(8,128)(2,1)} %pad_maximum_fusion.4), calls=%async_computation.9 | async-start | bytes 2359296 | tf_op jit(solution)/shard_map/all_to_all | solution.py:743
  936.5 121.0 %all-gather.26.cloned.1.call-start = ((), (), s32[]{:S(2)}) async-start(), calls=%async_computation.18 | async-start | bytes 3145728 | tf_op jit(solution)/shard_map/all_gather | solution.py:693
  969.1 53.2 %collective-permute-start.75 = (bf16[128,2048]{1,0:T(8,128)(2,1)}, bf16[128,2048]{1,0:T(8,128)(2,1)}, u32[]{:S(2)}, u32[]{:S(2)}) collective-permute-start(bf16[128,2048]{1,0:T(8,128)(2,1)} %get-tuple-element.327), channel_id=1, source_target_pairs={{0,8},{1,9},{2,10},{3,11},{4,12},{5,13},{6,14},{7,15},{8,0},{9,1},... | collective-permute-start | bytes 1572872 | tf_op jit(solution)/shard_map/routed/ppermute | solution.py:79
  970.9 51.4 %collective-permute-start.76 = (bf16[128,2048]{1,0:T(8,128)(2,1)}, bf16[128,2048]{1,0:T(8,128)(2,1)}, u32[]{:S(2)}, u32[]{:S(2)}) collective-permute-start(bf16[128,2048]{1,0:T(8,128)(2,1)} %fusion.60), channel_id=1, source_target_pairs={{0,4},{1,5},{2,6},{3,7},{4,8},{5,9},{6,10},{7,11},{8,12},{9,13},{1... | collective-permute-start | bytes 1572872 | tf_op jit(solution)/shard_map/routed/ppermute | solution.py:79
  981.1 45.2 %collective-permute-start.82 = (bf16[4,128,576]{1,2,0:T(8,128)(2,1)}, bf16[4,128,576]{1,2,0:T(8,128)(2,1)S(1)}, u32[]{:S(2)}, u32[]{:S(2)}) collective-permute-start(bf16[4,128,576]{1,2,0:T(8,128)(2,1)} %copy.294), channel_id=1, source_target_pairs={{1,0},{0,1},{3,2},{2,3},{5,4},{4,5},{7,6},{6,7},{9,8},{8,9},{11,10... | collective-permute-start | bytes 1769480 | tf_op jit(solution)/shard_map/grad_kv/ppermute | solution.py:75
  982.7 45.8 %collective-permute-start.83 = (bf16[4,128,576]{1,2,0:T(8,128)(2,1)}, bf16[4,128,576]{1,2,0:T(8,128)(2,1)S(1)}, u32[]{:S(2)}, u32[]{:S(2)}) collective-permute-start(bf16[4,128,576]{1,2,0:T(8,128)(2,1)} %copy.294), channel_id=1, source_target_pairs={{2,0},{3,1},{0,2},{1,3},{6,4},{7,5},{4,6},{5,7},{10,8},{11,9},{8,1... | collective-permute-start | bytes 1769480 | tf_op jit(solution)/shard_map/grad_kv/ppermute | solution.py:75
  987.5 45.7 %collective-permute-start.90 = (bf16[128,1024]{1,0:T(8,128)(2,1)S(1)}, bf16[128,1024]{1,0:T(8,128)(2,1)S(1)}, u32[]{:S(2)}, u32[]{:S(2)}) collective-permute-start(bf16[128,1024]{1,0:T(8,128)(2,1)S(1)} %get-tuple-element.490), channel_id=1, source_target_pairs={{0,4},{1,5},{2,6},{3,7},{4,8},{5,9},{6,10},{7,11},{8,12},{9,13},{1... | collective-permute-start | bytes 786440 | tf_op jit(solution)/shard_map/grad_output_w/ppermute | solution.py:79
  (175 other events, 4912.0 us)
Sparse Core Ops, SparseCore 0:
  9.6 18.6 all-gather.19
  29.8 17.1 all-gather.21
  48.6 17.1 all-gather.15
  446.0 91.8 all-gather.17
  539.3 9.0 all-gather.29
  573.2 11.8 reduce-scatter.7
  676.9 14.6 reduce-scatter.5
  721.6 16.3 reduce-scatter.3
  739.7 25.8 all-gather.23
  819.6 11.6 all-gather.27
  1043.4 12.6 all-gather.25
where the time goes:
time: 1080 us; the launch traced here: 1070 us
  waiting for transfers between devices  313 us (29%)
  Pallas kernels  244 us (23%)
  starting transfers between devices  165 us (15%)
  local copies, waits for them, and re-layouts  136 us (13%)
  other arithmetic  112 us (10%)
  matrix products  48.3 us (4%)
  blocking collectives  40.2 us (4%)
  between operations  16.4 us (2%)
    pallas_call x8, Pallas kernels, call(): pl.pallas_call(without_marks, out_shape=out_shape, in_specs=[pl.BlockSpec...  204 us
    ppermute x54, waiting for transfers between devices, pull(): return lax.ppermute(value, 'fsdp', perm)  166 us
    ppermute x36, waiting for transfers between devices, push(): return lax.ppermute(value, 'fsdp', partners(devices, q, k))  134 us
    ppermute x54, starting transfers between devices, pull(): return lax.ppermute(value, 'fsdp', perm)  71.1 us
    ppermute x36, starting transfers between devices, push(): return lax.ppermute(value, 'fsdp', partners(devices, q, k))  60.7 us
    dot_general x16, matrix products, contract(): return jnp.einsum(form, left, right, preferred_element_type=F32)  48.3 us
    unnamed x259, local copies, waits for them, and re-layouts  41 us
    pallas_call x2, Pallas kernels, weight_sums(): pl.pallas_call(functools.partial(weight_kernel, reps, len(marks)), grid=(...  39.6 us
  transfers between devices with their start and end apart: 111, of which 36 were waited for; matrix products, arithmetic and copies ran while one was open for 26% of the time, Pallas kernels for 17%

commit v1 on v0

--- a/solution.py
+++ b/solution.py
@@ -307,7 +307,7 @@
         for copy in loads[m]:
             copy.wait()
 
-        @pl.loop(0, 4)
+        @pl.loop(0, 4, unroll=2)
         def _(g):
             here = pl.ds(pl.multiple_of(g * span, span), span)
             value = rows_of(x, g * quarter, quarter).astype(F32)
@@ -339,7 +339,7 @@
                 copy.start()
         half_k = jnp.where(lane < DR, k_rot[m], jnp.zeros_like(k_rot[m]))
 
-        @pl.loop(0, 4)
+        @pl.loop(0, 4, unroll=2)
         def _(g):
             here = pl.ds(pl.multiple_of(g * span, span), span)
             scores = mm_t(q_nope[m, here, :], k_nope[m]) + mm_t(q_rot[m, here, :], half_k)
@@ -392,7 +392,7 @@
         grad_r[...] = jnp.zeros_like(grad_r)
         grad_v[...] = jnp.zeros_like(grad_v)
 
-        @pl.loop(0, 4)
+        @pl.loop(0, 4, unroll=2)
         def _(g):
             here = pl.ds(pl.multiple_of(g * span, span), span)
             above = jnp.concatenate(
@@ -476,11 +476,9 @@
         grad_shared[there, :] = mm_t(value, shared_down[...])
         whole[there, :] = value
 
-    chunks = down.shape[0] // 128
-
-    @pl.loop(0, chunks)
-    def _(f):
-        here = pl.ds(pl.multiple_of(f * 128, 128), 128)
+    total_rows = down.shape[0]
+    for start in range(0, total_rows, 512):
+        here = pl.ds(start, min(512, total_rows - start))
         grad_eh[:, here] = mm_t(back[...], down[here, :])
 
 
@@ -542,22 +540,27 @@
     for copy in loads:
         copy.wait()
 
-    @pl.loop(0, chunks)
+    def units(start, count):
+        value = mm_t(arrived[...], w[pl.ds(start, count * 256), :])
+        for j in range(count):
+            at = pl.multiple_of(start + j * 256, 256)
+            half = pl.multiple_of(start // 2 + j * 128, 128)
+            gate = value[:, j * 256 : j * 256 + 128]
+            lift = value[:, j * 256 + 128 : (j + 1) * 256]
+            sigma = 1.0 / (1.0 + jnp.exp(-gate))
+            grad = grad_eh[:, pl.ds(half, 128)]
+            hidden[:, pl.ds(half, 128)] = (gate * sigma * lift).astype(BF16)
+            grad_gu[:, pl.ds(at, 128)] = (
+                grad * lift * sigma * (1.0 + gate * (1.0 - sigma))
+            ).astype(BF16)
+            grad_gu[:, pl.ds(pl.multiple_of(at + 128, 128), 128)] = (grad * gate * sigma).astype(BF16)
+
+    @pl.loop(0, chunks // 2)
     def _(f):
-        rows = pl.ds(pl.multiple_of(f * 256, 256), 256)
-        cols = pl.ds(pl.multiple_of(f * 128, 128), 128)
-        value = mm_t(arrived[...], w[rows, :])
-        gate, lift = value[:, :128], value[:, 128:]
-        sigma = 1.0 / (1.0 + jnp.exp(-gate))
-        grad = grad_eh[:, cols]
-        hidden[:, cols] = (gate * sigma * lift).astype(BF16)
-        grad_gu[:, rows] = jnp.concatenate(
-            [
-                (grad * lift * sigma * (1.0 + gate * (1.0 - sigma))).astype(BF16),
-                (grad * gate * sigma).astype(BF16),
-            ],
-            axis=1,
-        )
+        units(pl.multiple_of(f * 512, 512), 2)
+
+    if chunks % 2:
+        units((chunks - 1) * 256, 1)
 
     spread_out(
         o, pick, 512,

time: 1080 us -> 1080 us (level)
  Pallas kernels: 244 us -> 230 us
  waiting for transfers between devices: 313 us -> 326 us
    pallas_call x8, Pallas kernels: 204 us -> 190 us  [call(): pl.pallas_call(without_marks, out_shape=out_shape, in_specs=[pl.BlockSpec...]
    ppermute x54, waiting for transfers between devices: 166 us -> 179 us  [pull(): return lax.ppermute(value, 'fsdp', perm)]
  transfers between devices with their start and end apart: 111 -> 111, of which waited for: 36 -> 37; matrix products, arithmetic and copies ran while one was open for 26% -> 26% of each run, Pallas kernels for 17% -> 16%
where the time goes in v1:
time: 1080 us; the launch traced here: 1070 us
  waiting for transfers between devices  326 us (30%)
  Pallas kernels  230 us (21%)
  starting transfers between devices  164 us (15%)
  local copies, waits for them, and re-layouts  136 us (13%)
  other arithmetic  112 us (10%)
  matrix products  48.3 us (4%)
  blocking collectives  39.4 us (4%)
  between operations  16.4 us (2%)
    pallas_call x8, Pallas kernels, call(): pl.pallas_call(without_marks, out_shape=out_shape, in_specs=[pl.BlockSpec...  190 us
    ppermute x54, waiting for transfers between devices, pull(): return lax.ppermute(value, 'fsdp', perm)  179 us
    ppermute x36, waiting for transfers between devices, push(): return lax.ppermute(value, 'fsdp', partners(devices, q, k))  134 us
    ppermute x54, starting transfers between devices, pull(): return lax.ppermute(value, 'fsdp', perm)  70.5 us
    ppermute x36, starting transfers between devices, push(): return lax.ppermute(value, 'fsdp', partners(devices, q, k))  60.7 us
    dot_general x16, matrix products, contract(): return jnp.einsum(form, left, right, preferred_element_type=F32)  48.3 us
    unnamed x259, local copies, waits for them, and re-layouts  41 us
    pallas_call x2, Pallas kernels, weight_sums(): pl.pallas_call(functools.partial(weight_kernel, reps, len(marks)), grid=(...  39.6 us
  transfers between devices with their start and end apart: 111, of which 37 were waited for; matrix products, arithmetic and copies ran while one was open for 26% of the time, Pallas kernels for 16%

profile of v1, /device:TPU:0, one launch (start us, length us, event | category | flops | bytes accessed | tf_op | source)
XLA Modules:
  0.0 1071.5 jit_solution(1617069301817646653)
XLA Ops:
  9.2 5.1 collective-permute-start.15
  20.7 6.7 all-to-all-start
  47.3 17.6 %collective-permute-done.18 = bf16[4,128,640]{1,2,0:T(8,128)(2,1)S(1)} collective-permute-done((bf16[4,128,640]{1,2,0:T(8,128)(2,1)S(1)}, bf16[4,128,640]{1,2,0:T(8,128)(2,1)S(1)}, u32[]{:S(2)}, u32[]{:S(2)}) %collective-permute-start.18) | collective-permute-done | bytes 655392 | tf_op jit(solution)/shard_map/small/ppermute | solution.py:75
  67.0 28.6 %collective-permute-done.1 = bf16[128,2048]{1,0:T(8,128)(2,1)S(1)} collective-permute-done((bf16[128,2048]{1,0:T(8,128)(2,1)S(1)}, bf16[128,2048]{1,0:T(8,128)(2,1)S(1)}, u32[]{:S(2)}, u32[]{:S(2)}) %collective-permute-start.1) | collective-permute-done | bytes 524320 | tf_op jit(solution)/shard_map/hidden/ppermute | solution.py:75
  99.6 7.0 collective-permute-done.21
  127.0 9.5 collective-permute-done.7
  150.5 5.0 fusion.123
  159.4 6.3 pad_maximum_fusion
  179.1 5.8 collective-permute-done.22.refs_10_.refs_9_
  185.9 30.0 %shard_map.307 = (bf16[16,128,128]{2,1,0:T(8,128)(2,1)}, bf16[2,1024,128]{2,1,0:T(8,128)(2,1)}, bf16[2,1024,128]{2,1,0:T(8,128)(2,1)}, bf16[2,1024,128]{2,1,0:T(...) custom-call(s32[16]{0:T(128)} %copy-done.93, ...), custom_call_target="tpu_custom_call" | custom-call | flops 9663676416 | bytes 21184512 | tf_op jit(solution)/shard_map/pallas_call | solution.py:250
  215.9 6.5 all-to-all-start.1
  231.6 11.4 %collective-permute-done.8 = bf16[128,2048]{1,0:T(8,128)(2,1)S(1)} collective-permute-done((bf16[128,2048]{1,0:T(8,128)(2,1)S(1)}, bf16[128,2048]{1,0:T(8,128)(2,1)S(1)}, u32[]{:S(2)}, u32[]{:S(2)}) %collective-permute-start.8) | collective-permute-done | bytes 524320 | tf_op jit(solution)/shard_map/cotangent/ppermute | solution.py:75
  273.5 4.4 all-to-all-start.2
  278.0 28.4 %collective-permute-done.33 = bf16[128,2048]{1,0:T(8,128)(2,1)} collective-permute-done((bf16[128,2048]{1,0:T(8,128)(2,1)S(1)}, bf16[128,2048]{1,0:T(8,128)(2,1)}, u32[]{:S(2)}, u32[]{:S(2)}) %collective-permute-start.33) | collective-permute-done | bytes 524320 | tf_op jit(solution)/shard_map/cotangent/ppermute | solution.py:75
  319.6 19.1 %collective-permute-done.36.refs_3_ = bf16[2,128,2048]{2,1,0:T(8,128)(2,1)S(1)} collective-permute-done((bf16[2,128,2048]{2,1,0:T(8,128)(2,1)}, bf16[2,128,2048]{2,1,0:T(8,128)(2,1)S(1)}, u32[]{:S(2)}, u32[]{:S(2)}) %collective-permute-start.36) | collective-permute-done | bytes 1048608 | tf_op jit(solution)/shard_map/cotangent/ppermute | solution.py:75
  341.6 5.9 collective-permute-done.38.refs_6_
  356.8 7.5 collective-permute-done.40.refs_8_
  365.5 13.9 %shard_map.308 = (bf16[576,2048]{1,0:T(8,128)(2,1)}, f32[576,1408]{1,0:T(8,128)}, f32[1024,176]{1,0:T(8,128)}, bf16[1024,2048]{1,0:T(8,128)(2,1)}) custom-call(bf16[2,128,2048]{2,1,0:T(8,128)(2,1)} %copy-done.15, bf16[2,128,2048]{2,1,0:T(8,128)(2,1)} %pad_maximum_fusion.13.refs_1_, bf16[2,128,2048]{2,1,0:T(8,128)(2,1)} %collective-permute-done.34.refs_2_, ...), custom_call_target="tpu_custom_call" | custom-call | flops 3925868544 | bytes 19759104 | tf_op jit(solution)/shard_map/pallas_call | solution.py:250
  379.4 13.5 %collective-permute-done.29 = bf16[128,2048]{1,0:T(8,128)(2,1)S(1)} collective-permute-done((bf16[128,2048]{1,0:T(8,128)(2,1)S(1)}, bf16[128,2048]{1,0:T(8,128)(2,1)S(1)}, u32[]{:S(2)}, u32[]{:S(2)}) %collective-permute-start.29) | collective-permute-done | bytes 524320 | tf_op jit(solution)/shard_map/mixed/ppermute | solution.py:75
  401.6 13.8 %shard_map.309 = (bf16[576,2048]{1,0:T(8,128)(2,1)}, f32[576,1408]{1,0:T(8,128)}, f32[1024,176]{1,0:T(8,128)}, bf16[1024,2048]{1,0:T(8,128)(2,1)}) custom-call(bf16[2,128,2048]{2,1,0:T(8,128)(2,1)} %copy-done.15, bf16[2,128,2048]{2,1,0:T(8,128)(2,1)} %pad_maximum_fusion.13.refs_1_, bf16[2,128,2048]{2,1,0:T(8,128)(2,1)} %collective-permute-done.34.refs_2_, ...), custom_call_target="tpu_custom_call" | custom-call | flops 3925868544 | bytes 19759104 | tf_op jit(solution)/shard_map/pallas_call | solution.py:250
  422.2 7.5 collective-permute-done.44.refs_6_
  434.0 9.4 collective-permute-done.46.refs_8_
  448.0 39.6 %shard_map.310 = (bf16[1024,2048]{1,0:T(8,128)(2,1)}, bf16[576,2048]{1,0:T(8,128)(2,1)}, bf16[576,1408]{1,0:T(8,128)(2,1)}, bf16[576,2816]{1,0:T(8,128)(2,1)}, b...) custom-call(bf16[2,128,2048]{2,1,0:T(8,128)(2,1)} %pad_maximum_fusio, ...), custom_call_target="tpu_custom_call" | custom-call | flops 17582522368 | bytes 32227328 | tf_op jit(solution)/shard_map/pallas_call | solution.py:250
  487.6 39.1 %shard_map.311 = (bf16[1024,2048]{1,0:T(8,128)(2,1)}, bf16[576,2048]{1,0:T(8,128)(2,1)}, bf16[576,1408]{1,0:T(8,128)(2,1)}, bf16[576,2816]{1,0:T(8,128)(2,1)}, b...) custom-call(bf16[2,128,2048]{2,1,0:T(8,128)(2,1)} %pad_maximum_fusio, ...), custom_call_target="tpu_custom_call", output_to_operand_aliasing={{7}: (16, {}), {8}: (17, {}), {9}: (18, {}), {10}: (19, {})... | custom-call | flops 17582522368 | bytes 32227328 | tf_op jit(solution)/shard_map/pallas_call | solution.py:250
  542.9 13.2 %shard_map.312 = (bf16[2,128,2048]{2,1,0:T(8,128)(2,1)}, bf16[2,128,2048]{2,1,0:T(8,128)(2,1)}, bf16[2,128,2048]{2,1,0:T(8,128)(2,1)}, bf16[2,128,2048]{2,1,0:T(...) custom-call(bf16[576,1408]{1,0:T(8,128)(2,1)} %get-tuple-element.251, ...), custom_call_target="tpu_custom_call" | custom-call | flops 5469372416 | bytes 11583488 | tf_op jit(solution)/shard_map/pallas_call | solution.py:250
  556.1 15.4 %shard_map.313.refs_17_ = bf16[2,704,2048]{2,1,0:T(8,128)(2,1)} custom-call(bf16[2,128,2048]{2,1,0:T(8,128)(2,1)} %fusion.50.refs_0_, bf16[2,128,2048]{2,1,0:T(8,128)(2,1)} %get-tuple-element.255.refs_1_.refs_6_, bf16[576,1408]{1,0:T(8,128)(2,1)} %get-tuple-element.251.refs_0_.refs_2_, bf16[576,1408]{1,0:T(8,128)(2,1)} %get-tuple-element.249.refs_3_.refs_0_, ...), custom_call_target="tpu_custom_call" | custom-call | flops 6643777536 | bytes 28835840 | tf_op jit(solution)/shard_map/pallas_call | solution.py:663
  575.4 11.4 %collective-permute-done.50 = bf16[1,128,2048]{2,1,0:T(8,128)(2,1)S(1)} collective-permute-done((bf16[1,128,2048]{2,1,0:T(8,128)(2,1)}, bf16[1,128,2048]{2,1,0:T(8,128)(2,1)S(1)}, u32[]{:S(2)}, u32[]{:S(2)}) %collective-permute-start.50) | collective-permute-done | bytes 524320 | tf_op jit(solution)/shard_map/grad_mixed/ppermute | solution.py:79
  594.3 14.9 %collective-permute-done.49 = bf16[2,128,2048]{2,1,0:T(8,128)(2,1)S(1)} collective-permute-done((bf16[2,128,2048]{2,1,0:T(8,128)(2,1)}, bf16[2,128,2048]{2,1,0:T(8,128)(2,1)S(1)}, u32[]{:S(2)}, u32[]{:S(2)}) %collective-permute-start.49) | collective-permute-done | bytes 1048608 | tf_op jit(solution)/shard_map/grad_mixed/ppermute | solution.py:79
  609.2 5.8 collective-permute-done.51
  616.7 10.7 %collective-permute-done.54 = bf16[2,128,2048]{2,1,0:T(8,128)(2,1)S(1)} collective-permute-done((bf16[2,128,2048]{2,1,0:T(8,128)(2,1)}, bf16[2,128,2048]{2,1,0:T(8,128)(2,1)S(1)}, u32[]{:S(2)}, u32[]{:S(2)}) %collective-permute-start.54) | collective-permute-done | bytes 1048608 | tf_op jit(solution)/shard_map/grad_mixed/ppermute | solution.py:79
  628.6 12.2 %shard_map.314 = (bf16[2,128,2048]{2,1,0:T(8,128)(2,1)}, bf16[2,128,2048]{2,1,0:T(8,128)(2,1)}, bf16[2,128,2048]{2,1,0:T(8,128)(2,1)}, bf16[2,128,2048]{2,1,0:T(...) custom-call(bf16[576,1408]{1,0:T(8,128)(2,1)} %get-tuple-element.249, ...), custom_call_target="tpu_custom_call", output_to_operand_aliasing={{0}: (6, {}), {1}: (7, {}), {2}: (8, {}), {3}: (9, {}), {4}... | custom-call | flops 5469372416 | bytes 11583488 | tf_op jit(solution)/shard_map/pallas_call | solution.py:250
  640.8 7.1 collective-permute-done.57
  650.6 24.2 %shard_map.315 = (bf16[2,704,2048]{2,1,0:T(8,128)(2,1)}, bf16[2,704,2048]{2,1,0:T(8,128)(2,1)}) custom-call(f32[128,2048]{1,0:T(8,128)} %get-tuple-element.455.refs_0_, bf16[2,128,2048]{2,1,0:T(8,128)(2,1)} %get-tuple-element.275.refs_1_, bf16[576,2816]{1,0:T(8,128)(2,1)} %get-tuple-element.284.refs_2_, bf16[576,2816]{1,0:T(8,128)(2,1)} %get-tuple-element.285.refs_3_, ...), custom_call_target="tpu_custom_call" | custom-call | flops 13287555072 | bytes 28835840 | tf_op jit(solution)/shard_map/pallas_call | solution.py:663
  675.0 4.4 fusion.40
  681.6 37.1 %all_to_all.35 = bf16[16,128,352]{1,2,0:T(8,128)(2,1)} all-to-all(bf16[16,128,352]{1,2,0:T(8,128)(2,1)S(1)} %bitcast.381), channel_id=1, replica_groups=mesh['rep'=2,'fsdp'=16] {'fsdp'}, dimensions={0} | all-to-all | bytes 2883584 | tf_op jit(solution)/shard_map/all_to_all | solution.py:746
  744.9 4.5 add_convert_fusion
  752.5 7.8 all-to-all-done.4.refs_11_
  762.8 28.3 %shard_map.316 = (bf16[16,128,256]{2,1,0:T(8,128)(2,1)}, bf16[4,128,640]{2,1,0:T(8,128)(2,1)}, bf16[4,128,640]{2,1,0:T(8,128)(2,1)}, bf16[4,128,640]{2,1,0:T(8,1...) custom-call(s32[16]{0:T(128)} %copy-done.93, ...), custom_call_target="tpu_custom_call" | custom-call | flops 8589934592 | bytes 30212096 | tf_op jit(solution)/shard_map/pallas_call | solution.py:250
  805.3 4.7 all-to-all-start.5
  822.7 23.3 %collective-permute-done.63 = bf16[1,128,2048]{2,1,0:T(8,128)(2,1)} collective-permute-done((bf16[1,128,2048]{2,1,0:T(8,128)(2,1)}, bf16[1,128,2048]{2,1,0:T(8,128)(2,1)}, u32[]{:S(2)}, u32[]{:S(2)}) %collective-permute-start.63) | collective-permute-done | bytes 524320 | tf_op jit(solution)/shard_map/routed/ppermute | solution.py:79
  855.9 6.4 collective-permute-done.68
  865.0 19.8 %collective-permute-done.64 = bf16[2,128,2048]{2,1,0:T(8,128)(2,1)S(1)} collective-permute-done((bf16[2,128,2048]{2,1,0:T(8,128)(2,1)S(1)}, bf16[2,128,2048]{2,1,0:T(8,128)(2,1)S(1)}, u32[]{:S(2)}, u32[]{:S(2)}) %collective-permute-start.64) | collective-permute-done | bytes 1048608 | tf_op jit(solution)/shard_map/routed/ppermute | solution.py:79
  893.2 13.3 %collective-permute-done.60 = bf16[2,128,2048]{2,1,0:T(8,128)(2,1)} collective-permute-done((bf16[2,128,2048]{2,1,0:T(8,128)(2,1)}, bf16[2,128,2048]{2,1,0:T(8,128)(2,1)}, u32[]{:S(2)}, u32[]{:S(2)}) %collective-permute-start.60) | collective-permute-done | bytes 1048608 | tf_op jit(solution)/shard_map/routed/ppermute | solution.py:79
  927.9 5.5 all-to-all-start.6
  935.5 5.0 fusion
  940.6 6.1 fusion.30
  984.5 22.1 %collective-permute-start.90 = (bf16[128,1024]{1,0:T(8,128)(2,1)S(1)}, bf16[128,1024]{1,0:T(8,128)(2,1)S(1)}, u32[]{:S(2)}, u32[]{:S(2)}) collective-permute-start(bf16[128,1024]{1,0:T(8,128)(2,1)S(1)} %get-tuple-element.490), channel_id=1, source_target_pairs={{0,4},{1,5},{2,6},{3,7},{4,8},{5,9},{6,10},{7,11},{8,12},{9,13},{1... | collective-permute-start | bytes 786440 | tf_op jit(solution)/shard_map/grad_output_w/ppermute | solution.py:79
  1006.6 12.8 %collective-permute-done.75 = bf16[128,2048]{1,0:T(8,128)(2,1)} collective-permute-done((bf16[128,2048]{1,0:T(8,128)(2,1)}, bf16[128,2048]{1,0:T(8,128)(2,1)}, u32[]{:S(2)}, u32[]{:S(2)}) %collective-permute-start.75) | collective-permute-done | bytes 524320 | tf_op jit(solution)/shard_map/routed/ppermute | solution.py:79
  (693 shorter events, 397.2 us)
Async XLA Ops:
  7.2 143.3 %all-gather.20.cloned.1.call-start = ((), (), s32[]{:S(2)}) async-start(), calls=%async_computation.15 | async-start | bytes 8650752 | tf_op jit(solution)/shard_map/all_gather | solution.py:813
  7.9 147.6 %all-gather.22.cloned.1.call-start = ((), (), s32[]{:S(2)}) async-start(), calls=%async_computation.16 | async-start | bytes 8650752 | tf_op jit(solution)/shard_map/all_gather | solution.py:813
  18.2 48.2 %collective-permute-start = (bf16[128,2048]{1,0:T(8,128)(2,1)S(1)}, bf16[128,2048]{1,0:T(8,128)(2,1)}, u32[]{:S(2)}, u32[]{:S(2)}) collective-permute-start(bf16[128,2048]{1,0:T(8,128)(2,1)S(1)} %bitcast.371), channel_id=1, source_target_pairs={{12,0},{13,1},{14,2},{15,3},{0,4},{1,5},{2,6},{3,7},{4,8},{5,9},{6... | collective-permute-start | bytes 1572872 | tf_op jit(solution)/shard_map/hidden/ppermute | solution.py:75
  20.7 118.0 %all-to-all-start = ((bf16[16,128,256]{1,2,0:T(8,128)(2,1)}), bf16[16,128,256]{1,2,0:T(8,128)(2,1)}, u32[]{:S(2)}, u32[]{:S(2)}) async-start(bf16[16,128,256]{1,2,0:T(8,128)(2,1)} %pad_maximum_fusion.9), calls=%async_computation | async-start | bytes 2097152 | tf_op jit(solution)/shard_map/all_to_all | solution.py:746
  27.4 138.3 %all-gather.16.cloned.1.call-start = ((), (), s32[]{:S(2)}) async-start(), calls=%async_computation.10 | async-start | bytes 8650752 | tf_op jit(solution)/shard_map/all_gather | solution.py:813
  38.7 57.0 %collective-permute-start.1 = (bf16[128,2048]{1,0:T(8,128)(2,1)S(1)}, bf16[128,2048]{1,0:T(8,128)(2,1)S(1)}, u32[]{:S(2)}, u32[]{:S(2)}) collective-permute-start(bf16[128,2048]{1,0:T(8,128)(2,1)S(1)} %bitcast.372), channel_id=1, source_target_pairs={{8,0},{9,1},{10,2},{11,3},{12,4},{13,5},{14,6},{15,7},{0,8},{1,9},... | collective-permute-start | bytes 1572872 | tf_op jit(solution)/shard_map/hidden/ppermute | solution.py:75
  43.1 54.7 %collective-permute-start.19 = (bf16[4,128,640]{1,2,0:T(8,128)(2,1)S(1)}, bf16[4,128,640]{1,2,0:T(8,128)(2,1)S(1)}, u32[]{:S(2)}, u32[]{:S(2)}) collective-permute-start(bf16[4,128,640]{1,2,0:T(8,128)(2,1)S(1)} %pad_maximum_fusion.15), channel_id=1, source_target_pairs={{2,0},{3,1},{0,2},{1,3},{6,4},{7,5},{4,6},{5,7},{10,8},{11,9},{8,1... | collective-permute-start | bytes 1966088 | tf_op jit(solution)/shard_map/small/ppermute | solution.py:75
  46.8 68.4 %collective-permute-start.3 = (bf16[2,128,2048]{2,1,0:T(8,128)(2,1)}, bf16[2,128,2048]{2,1,0:T(8,128)(2,1)}, u32[]{:S(2)}, u32[]{:S(2)}) collective-permute-start(bf16[2,128,2048]{2,1,0:T(8,128)(2,1)} %pad_maximum_fusion.6.refs_2_.refs_1_), channel_id=1, source_target_pairs={{1,0},{0,1},{3,2},{2,3},{5,4},{4,5},{7,6},{6,7},{9,8},{8,9},{11,10... | collective-permute-start | bytes 3145736 | tf_op jit(solution)/shard_map/hidden/ppermute | solution.py:75
  64.9 50.3 %collective-permute-start.4 = (bf16[2,128,2048]{2,1,0:T(8,128)(2,1)}, bf16[2,128,2048]{2,1,0:T(8,128)(2,1)}, u32[]{:S(2)}, u32[]{:S(2)}) collective-permute-start(bf16[2,128,2048]{2,1,0:T(8,128)(2,1)} %pad_maximum_fusion.6.refs_2_.refs_1_), channel_id=1, source_target_pairs={{2,0},{3,1},{0,2},{1,3},{6,4},{7,5},{4,6},{5,7},{10,8},{11,9},{8,1... | collective-permute-start | bytes 3145736 | tf_op jit(solution)/shard_map/hidden/ppermute | solution.py:75
  136.5 35.5 %collective-permute-start.13 = (bf16[1,128,2048]{2,1,0:T(8,128)(2,1)}, bf16[1,128,2048]{2,1,0:T(8,128)(2,1)}, u32[]{:S(2)}, u32[]{:S(2)}) collective-permute-start(bf16[1,128,2048]{2,1,0:T(8,128)(2,1)} %slice.562), channel_id=1, source_target_pairs={{2,0},{3,1},{0,2},{1,3},{6,4},{7,5},{4,6},{5,7},{10,8},{11,9},{8,1... | collective-permute-start | bytes 1572872 | tf_op jit(solution)/shard_map/hidden/ppermute | solution.py:75
  137.0 35.0 %collective-permute-start.14 = (bf16[1,128,2048]{2,1,0:T(8,128)(2,1)}, bf16[1,128,2048]{2,1,0:T(8,128)(2,1)}, u32[]{:S(2)}, u32[]{:S(2)}) collective-permute-start(bf16[1,128,2048]{2,1,0:T(8,128)(2,1)} %slice.563), channel_id=1, source_target_pairs={{1,0},{0,1},{3,2},{2,3},{5,4},{4,5},{7,6},{6,7},{9,8},{8,9},{11,10... | collective-permute-start | bytes 1572872 | tf_op jit(solution)/shard_map/hidden/ppermute | solution.py:75
  254.1 52.3 %collective-permute-start.33 = (bf16[128,2048]{1,0:T(8,128)(2,1)S(1)}, bf16[128,2048]{1,0:T(8,128)(2,1)}, u32[]{:S(2)}, u32[]{:S(2)}) collective-permute-start(bf16[128,2048]{1,0:T(8,128)(2,1)S(1)} %bitcast.377), channel_id=1, source_target_pairs={{8,0},{9,1},{10,2},{11,3},{12,4},{13,5},{14,6},{15,7},{0,8},{1,9},... | collective-permute-start | bytes 1572872 | tf_op jit(solution)/shard_map/cotangent/ppermute | solution.py:75
  256.2 52.5 %collective-permute-start.34 = (bf16[2,128,2048]{2,1,0:T(8,128)(2,1)S(1)}, bf16[2,128,2048]{2,1,0:T(8,128)(2,1)}, u32[]{:S(2)}, u32[]{:S(2)}) collective-permute-start(bf16[2,128,2048]{2,1,0:T(8,128)(2,1)S(1)} %pad_maximum_fusion.8.refs_0_), channel_id=1, source_target_pairs={{1,0},{0,1},{3,2},{2,3},{5,4},{4,5},{7,6},{6,7},{9,8},{8,9},{11,10... | collective-permute-start | bytes 3145736 | tf_op jit(solution)/shard_map/cotangent/ppermute | solution.py:75
  256.7 51.9 %collective-permute-start.35 = (bf16[2,128,2048]{2,1,0:T(8,128)(2,1)S(1)}, bf16[2,128,2048]{2,1,0:T(8,128)(2,1)}, u32[]{:S(2)}, u32[]{:S(2)}) collective-permute-start(bf16[2,128,2048]{2,1,0:T(8,128)(2,1)S(1)} %pad_maximum_fusion.8.refs_0_), channel_id=1, source_target_pairs={{2,0},{3,1},{0,2},{1,3},{6,4},{7,5},{4,6},{5,7},{10,8},{11,9},{8,1... | collective-permute-start | bytes 3145736 | tf_op jit(solution)/shard_map/cotangent/ppermute | solution.py:75
  273.5 119.6 %all-to-all-start.2 = ((bf16[16,128,352]{1,2,0:T(8,128)(2,1)}), bf16[16,128,352]{1,2,0:T(8,128)(2,1)}, u32[]{:S(2)}, u32[]{:S(2)}) async-start(bf16[16,128,352]{1,2,0:T(8,128)(2,1)} %pad_maximum_fusion.3), calls=%async_computation.2 | async-start | bytes 2883584 | tf_op jit(solution)/shard_map/all_to_all | solution.py:746
  277.9 440.9 %all-gather.18.cloned.1.call-start = ((), (), s32[]{:S(2)}) async-start(), calls=%async_computation.11 | async-start | bytes 6684672 | tf_op jit(solution)/shard_map/all_gather | solution.py:906
  312.4 35.0 %collective-permute-start.38 = (bf16[1,128,2048]{2,1,0:T(8,128)(2,1)}, bf16[1,128,2048]{2,1,0:T(8,128)(2,1)}, u32[]{:S(2)}, u32[]{:S(2)}) collective-permute-start(bf16[1,128,2048]{2,1,0:T(8,128)(2,1)} %slice.585), channel_id=1, source_target_pairs={{2,0},{3,1},{0,2},{1,3},{6,4},{7,5},{4,6},{5,7},{10,8},{11,9},{8,1... | collective-permute-start | bytes 1572872 | tf_op jit(solution)/shard_map/cotangent/ppermute | solution.py:75
  315.1 34.0 %collective-permute-start.39 = (bf16[1,128,2048]{2,1,0:T(8,128)(2,1)}, bf16[1,128,2048]{2,1,0:T(8,128)(2,1)}, u32[]{:S(2)}, u32[]{:S(2)}) collective-permute-start(bf16[1,128,2048]{2,1,0:T(8,128)(2,1)} %slice.586), channel_id=1, source_target_pairs={{1,0},{0,1},{3,2},{2,3},{5,4},{4,5},{7,6},{6,7},{9,8},{8,9},{11,10... | collective-permute-start | bytes 1572872 | tf_op jit(solution)/shard_map/cotangent/ppermute | solution.py:75
  316.6 34.0 %collective-permute-start.27 = (bf16[128,2048]{1,0:T(8,128)(2,1)}, bf16[128,2048]{1,0:T(8,128)(2,1)}, u32[]{:S(2)}, u32[]{:S(2)}) collective-permute-start(bf16[128,2048]{1,0:T(8,128)(2,1)} %multiply_convert_fusion.1.refs_14_), channel_id=1, source_target_pairs={{4,0},{5,1},{6,2},{7,3},{8,4},{9,5},{10,6},{11,7},{12,8},{13,9},{1... | collective-permute-start | bytes 1572872 | tf_op jit(solution)/shard_map/mixed/ppermute | solution.py:75
  352.9 40.1 %collective-permute-start.30 = (bf16[2,128,2048]{2,1,0:T(8,128)(2,1)}, bf16[2,128,2048]{2,1,0:T(8,128)(2,1)}, u32[]{:S(2)}, u32[]{:S(2)}) collective-permute-start(bf16[2,128,2048]{2,1,0:T(8,128)(2,1)} %pad_maximum_fusion.11.refs_0_), channel_id=1, source_target_pairs={{1,0},{0,1},{3,2},{2,3},{5,4},{4,5},{7,6},{6,7},{9,8},{8,9},{11,10... | collective-permute-start | bytes 3145736 | tf_op jit(solution)/shard_map/mixed/ppermute | solution.py:75
  354.6 38.4 %collective-permute-start.31 = (bf16[2,128,2048]{2,1,0:T(8,128)(2,1)}, bf16[2,128,2048]{2,1,0:T(8,128)(2,1)}, u32[]{:S(2)}, u32[]{:S(2)}) collective-permute-start(bf16[2,128,2048]{2,1,0:T(8,128)(2,1)} %pad_maximum_fusion.11.refs_0_), channel_id=1, source_target_pairs={{2,0},{3,1},{0,2},{1,3},{6,4},{7,5},{4,6},{5,7},{10,8},{11,9},{8,1... | collective-permute-start | bytes 3145736 | tf_op jit(solution)/shard_map/mixed/ppermute | solution.py:75
  444.2 286.4 %all-gather.30.cloned.1.call-start = ((), (), s32[]{:S(2)}) async-start(), calls=%async_computation.20 | async-start | bytes 2162688 | tf_op jit(solution)/shard_map/all_gather | solution.py:696
  535.1 225.3 %reduce-scatter.8.cloned.1.call-start = ((), (), s32[]{:S(2)}) async-start(), calls=%async_computation.14 | async-start | bytes 8650752 | tf_op jit(solution)/shard_map/reduce_scatter | solution.py:957
  571.6 188.8 %reduce-scatter.6.cloned.1.call-start = ((), (), s32[]{:S(2)}) async-start(), calls=%async_computation.13 | async-start | bytes 8650752 | tf_op jit(solution)/shard_map/reduce_scatter | solution.py:957
  574.5 34.7 %collective-permute-start.49 = (bf16[2,128,2048]{2,1,0:T(8,128)(2,1)}, bf16[2,128,2048]{2,1,0:T(8,128)(2,1)S(1)}, u32[]{:S(2)}, u32[]{:S(2)}) collective-permute-start(bf16[2,128,2048]{2,1,0:T(8,128)(2,1)} %fusion.48.refs_6_), channel_id=1, source_target_pairs={{0,1},{1,0},{2,3},{3,2},{4,5},{5,4},{6,7},{7,6},{8,9},{9,8},{10,11... | collective-permute-start | bytes 3145736 | tf_op jit(solution)/shard_map/grad_mixed/ppermute | solution.py:79
  592.1 35.3 %collective-permute-start.54 = (bf16[2,128,2048]{2,1,0:T(8,128)(2,1)}, bf16[2,128,2048]{2,1,0:T(8,128)(2,1)S(1)}, u32[]{:S(2)}, u32[]{:S(2)}) collective-permute-start(bf16[2,128,2048]{2,1,0:T(8,128)(2,1)} %fusion.51), channel_id=1, source_target_pairs={{0,1},{1,0},{2,3},{3,2},{4,5},{5,4},{6,7},{7,6},{8,9},{9,8},{10,11... | collective-permute-start | bytes 3145736 | tf_op jit(solution)/shard_map/grad_mixed/ppermute | solution.py:79
  593.6 34.7 %collective-permute-start.55 = (bf16[2,128,2048]{2,1,0:T(8,128)(2,1)S(1)}, bf16[2,128,2048]{2,1,0:T(8,128)(2,1)S(1)}, u32[]{:S(2)}, u32[]{:S(2)}) collective-permute-start(bf16[2,128,2048]{2,1,0:T(8,128)(2,1)S(1)} %copy-done.73), channel_id=1, source_target_pairs={{0,2},{1,3},{2,0},{3,1},{4,6},{5,7},{6,4},{7,5},{8,10},{9,11},{10,... | collective-permute-start | bytes 3145736 | tf_op jit(solution)/shard_map/grad_mixed/ppermute | solution.py:79
  674.9 85.5 %reduce-scatter.4.cloned.1.call-start = ((), (), s32[]{:S(2)}) async-start(), calls=%async_computation.12 | async-start | bytes 8650752 | tf_op jit(solution)/shard_map/reduce_scatter | solution.py:957
  718.7 44.1 %all-gather.24.cloned.1.call-start = ((), (), s32[]{:S(2)}) async-start(), calls=%async_computation.17 | async-start | bytes 18874368 | tf_op jit(solution)/shard_map/all_gather | solution.py:955
  805.3 82.3 %all-to-all-start.5 = ((bf16[16,128,256]{2,1,0:T(8,128)(2,1)}), bf16[16,128,256]{2,1,0:T(8,128)(2,1)S(1)}, u32[]{:S(2)}, u32[]{:S(2)}) async-start(bf16[16,128,256]{2,1,0:T(8,128)(2,1)} %get-tuple-element.324), calls=%async_computation.8 | async-start | bytes 2097152 | tf_op jit(solution)/shard_map/all_to_all | solution.py:746
  810.0 217.8 %all-gather.28.cloned.1.call-start = ((), (), s32[]{:S(2)}) async-start(), calls=%async_computation.19 | async-start | bytes 4325376 | tf_op jit(solution)/shard_map/all_gather | solution.py:696
  810.0 40.2 %collective-permute-start.59 = (bf16[1,128,2048]{2,1,0:T(8,128)(2,1)}, bf16[1,128,2048]{2,1,0:T(8,128)(2,1)}, u32[]{:S(2)}, u32[]{:S(2)}) collective-permute-start(bf16[1,128,2048]{2,1,0:T(8,128)(2,1)} %get-tuple-element.308), channel_id=1, source_target_pairs={{0,2},{1,3},{2,0},{3,1},{4,6},{5,7},{6,4},{7,5},{8,10},{9,11},{10,... | collective-permute-start | bytes 1572872 | tf_op jit(solution)/shard_map/routed/ppermute | solution.py:79
  812.0 41.2 %collective-permute-start.61 = (bf16[1,128,2048]{2,1,0:T(8,128)(2,1)}, bf16[1,128,2048]{2,1,0:T(8,128)(2,1)S(1)}, u32[]{:S(2)}, u32[]{:S(2)}) collective-permute-start(bf16[1,128,2048]{2,1,0:T(8,128)(2,1)} %get-tuple-element.310), channel_id=1, source_target_pairs={{0,1},{1,0},{2,3},{3,2},{4,5},{5,4},{6,7},{7,6},{8,9},{9,8},{10,11... | collective-permute-start | bytes 1572872 | tf_op jit(solution)/shard_map/routed/ppermute | solution.py:79
  819.5 42.8 %collective-permute-start.68 = (bf16[4,128,640]{2,1,0:T(8,128)(2,1)}, bf16[4,128,640]{2,1,0:T(8,128)(2,1)S(1)}, u32[]{:S(2)}, u32[]{:S(2)}) collective-permute-start(bf16[4,128,640]{2,1,0:T(8,128)(2,1)} %fusion.69), channel_id=1, source_target_pairs={{0,1},{1,0},{2,3},{3,2},{4,5},{5,4},{6,7},{7,6},{8,9},{9,8},{10,11... | collective-permute-start | bytes 1966088 | tf_op jit(solution)/shard_map/grad_latent/ppermute | solution.py:79
  848.3 36.5 %collective-permute-start.64 = (bf16[2,128,2048]{2,1,0:T(8,128)(2,1)S(1)}, bf16[2,128,2048]{2,1,0:T(8,128)(2,1)S(1)}, u32[]{:S(2)}, u32[]{:S(2)}) collective-permute-start(bf16[2,128,2048]{2,1,0:T(8,128)(2,1)S(1)} %fusion.56), channel_id=1, source_target_pairs={{0,1},{1,0},{2,3},{3,2},{4,5},{5,4},{6,7},{7,6},{8,9},{9,8},{10,11... | collective-permute-start | bytes 3145736 | tf_op jit(solution)/shard_map/routed/ppermute | solution.py:79
  850.2 35.9 %collective-permute-start.66 = (bf16[2,128,2048]{2,1,0:T(8,128)(2,1)S(1)}, bf16[2,128,2048]{2,1,0:T(8,128)(2,1)S(1)}, u32[]{:S(2)}, u32[]{:S(2)}) collective-permute-start(bf16[2,128,2048]{2,1,0:T(8,128)(2,1)S(1)} %fusion.57), channel_id=1, source_target_pairs={{0,2},{1,3},{2,0},{3,1},{4,6},{5,7},{6,4},{7,5},{8,10},{9,11},{10,... | collective-permute-start | bytes 3145736 | tf_op jit(solution)/shard_map/routed/ppermute | solution.py:79
  853.3 53.2 %collective-permute-start.60 = (bf16[2,128,2048]{2,1,0:T(8,128)(2,1)}, bf16[2,128,2048]{2,1,0:T(8,128)(2,1)}, u32[]{:S(2)}, u32[]{:S(2)}) collective-permute-start(bf16[2,128,2048]{2,1,0:T(8,128)(2,1)} %fusion.54), channel_id=1, source_target_pairs={{0,1},{1,0},{2,3},{3,2},{4,5},{5,4},{6,7},{7,6},{8,9},{9,8},{10,11... | collective-permute-start | bytes 3145736 | tf_op jit(solution)/shard_map/routed/ppermute | solution.py:79
  862.3 44.4 %collective-permute-start.62 = (bf16[2,128,2048]{2,1,0:T(8,128)(2,1)}, bf16[2,128,2048]{2,1,0:T(8,128)(2,1)}, u32[]{:S(2)}, u32[]{:S(2)}) collective-permute-start(bf16[2,128,2048]{2,1,0:T(8,128)(2,1)} %fusion.55), channel_id=1, source_target_pairs={{0,2},{1,3},{2,0},{3,1},{4,6},{5,7},{6,4},{7,5},{8,10},{9,11},{10,... | collective-permute-start | bytes 3145736 | tf_op jit(solution)/shard_map/routed/ppermute | solution.py:79
  916.7 45.2 %collective-permute-start.79 = (bf16[128,576]{1,0:T(8,128)(2,1)}, bf16[128,576]{1,0:T(8,128)(2,1)}, u32[]{:S(2)}, u32[]{:S(2)}) collective-permute-start(bf16[128,576]{1,0:T(8,128)(2,1)} %pad_maximum_fusion.19), channel_id=1, source_target_pairs={{4,0},{5,1},{6,2},{7,3},{8,4},{9,5},{10,6},{11,7},{12,8},{13,9},{1... | collective-permute-start | bytes 442376 | tf_op jit(solution)/shard_map/grad_kv/ppermute | solution.py:75
  919.9 46.3 %collective-permute-start.80 = (bf16[128,576]{1,0:T(8,128)(2,1)}, bf16[128,576]{1,0:T(8,128)(2,1)}, u32[]{:S(2)}, u32[]{:S(2)}) collective-permute-start(bf16[128,576]{1,0:T(8,128)(2,1)} %pad_maximum_fusion.19), channel_id=1, source_target_pairs={{12,0},{13,1},{14,2},{15,3},{0,4},{1,5},{2,6},{3,7},{4,8},{5,9},{6... | collective-permute-start | bytes 442376 | tf_op jit(solution)/shard_map/grad_kv/ppermute | solution.py:75
  919.9 48.1 %collective-permute-start.81 = (bf16[128,576]{1,0:T(8,128)(2,1)}, bf16[128,576]{1,0:T(8,128)(2,1)}, u32[]{:S(2)}, u32[]{:S(2)}) collective-permute-start(bf16[128,576]{1,0:T(8,128)(2,1)} %pad_maximum_fusion.19), channel_id=1, source_target_pairs={{8,0},{9,1},{10,2},{11,3},{12,4},{13,5},{14,6},{15,7},{0,8},{1,9},... | collective-permute-start | bytes 442376 | tf_op jit(solution)/shard_map/grad_kv/ppermute | solution.py:75
  927.9 110.1 %all-to-all-start.6 = ((bf16[16,144,256]{2,1,0:T(8,128)(2,1)}), bf16[16,144,256]{2,1,0:T(8,128)(2,1)}, u32[]{:S(2)}, u32[]{:S(2)}) async-start(bf16[16,144,256]{2,1,0:T(8,128)(2,1)} %pad_maximum_fusion.4), calls=%async_computation.9 | async-start | bytes 2359296 | tf_op jit(solution)/shard_map/all_to_all | solution.py:746
  933.4 121.3 %all-gather.26.cloned.1.call-start = ((), (), s32[]{:S(2)}) async-start(), calls=%async_computation.18 | async-start | bytes 3145728 | tf_op jit(solution)/shard_map/all_gather | solution.py:696
  966.2 53.2 %collective-permute-start.75 = (bf16[128,2048]{1,0:T(8,128)(2,1)}, bf16[128,2048]{1,0:T(8,128)(2,1)}, u32[]{:S(2)}, u32[]{:S(2)}) collective-permute-start(bf16[128,2048]{1,0:T(8,128)(2,1)} %get-tuple-element.327), channel_id=1, source_target_pairs={{0,8},{1,9},{2,10},{3,11},{4,12},{5,13},{6,14},{7,15},{8,0},{9,1},... | collective-permute-start | bytes 1572872 | tf_op jit(solution)/shard_map/routed/ppermute | solution.py:79
  968.0 51.4 %collective-permute-start.76 = (bf16[128,2048]{1,0:T(8,128)(2,1)}, bf16[128,2048]{1,0:T(8,128)(2,1)}, u32[]{:S(2)}, u32[]{:S(2)}) collective-permute-start(bf16[128,2048]{1,0:T(8,128)(2,1)} %fusion.60), channel_id=1, source_target_pairs={{0,4},{1,5},{2,6},{3,7},{4,8},{5,9},{6,10},{7,11},{8,12},{9,13},{1... | collective-permute-start | bytes 1572872 | tf_op jit(solution)/shard_map/routed/ppermute | solution.py:79
  978.3 45.2 %collective-permute-start.82 = (bf16[4,128,576]{1,2,0:T(8,128)(2,1)}, bf16[4,128,576]{1,2,0:T(8,128)(2,1)S(1)}, u32[]{:S(2)}, u32[]{:S(2)}) collective-permute-start(bf16[4,128,576]{1,2,0:T(8,128)(2,1)} %copy.294), channel_id=1, source_target_pairs={{1,0},{0,1},{3,2},{2,3},{5,4},{4,5},{7,6},{6,7},{9,8},{8,9},{11,10... | collective-permute-start | bytes 1769480 | tf_op jit(solution)/shard_map/grad_kv/ppermute | solution.py:75
  979.7 45.9 %collective-permute-start.83 = (bf16[4,128,576]{1,2,0:T(8,128)(2,1)}, bf16[4,128,576]{1,2,0:T(8,128)(2,1)S(1)}, u32[]{:S(2)}, u32[]{:S(2)}) collective-permute-start(bf16[4,128,576]{1,2,0:T(8,128)(2,1)} %copy.294), channel_id=1, source_target_pairs={{2,0},{3,1},{0,2},{1,3},{6,4},{7,5},{4,6},{5,7},{10,8},{11,9},{8,1... | collective-permute-start | bytes 1769480 | tf_op jit(solution)/shard_map/grad_kv/ppermute | solution.py:75
  984.5 45.8 %collective-permute-start.90 = (bf16[128,1024]{1,0:T(8,128)(2,1)S(1)}, bf16[128,1024]{1,0:T(8,128)(2,1)S(1)}, u32[]{:S(2)}, u32[]{:S(2)}) collective-permute-start(bf16[128,1024]{1,0:T(8,128)(2,1)S(1)} %get-tuple-element.490), channel_id=1, source_target_pairs={{0,4},{1,5},{2,6},{3,7},{4,8},{5,9},{6,10},{7,11},{8,12},{9,13},{1... | collective-permute-start | bytes 786440 | tf_op jit(solution)/shard_map/grad_output_w/ppermute | solution.py:79
  (175 other events, 4883.7 us)
Sparse Core Ops, SparseCore 0:
  9.6 18.6 all-gather.19
  29.8 17.1 all-gather.21
  48.6 17.1 all-gather.15
  444.3 91.8 all-gather.17
  537.6 9.2 all-gather.29
  571.7 11.8 reduce-scatter.7
  675.0 14.3 reduce-scatter.5
  718.8 16.3 reduce-scatter.3
  736.9 25.8 all-gather.23
  816.3 11.6 all-gather.27
  1040.5 12.6 all-gather.25
